TPU v7x, 32 devices: a whole 2x2x4 slice. The times are simulated.
32 devices in a mesh: seq: 8 (over y, x, core), tp: 4 (over z).
Axes of the slice: x: 2, y: 2, z: 4, core: 2. Of those that a mesh axis runs over, the one named last changes fastest.
Arguments:
- tokens: bfloat16 [4096, 2048], P('seq'), may hold values from -6 to 6
- w_zx: float32 [2048, 8192], P(('seq', 'tp')), may hold values from -0.125 to 0.125
- w_dt: float32 [2048, 64], P(('seq', 'tp')), may hold values from -0.26516503 to 0.26516503
- w_bc: float32 [2048, 256], P(('seq', 'tp')), may hold values from -0.125 to 0.125
- conv_x_weight: float32 [4, 4096], P(None, 'tp'), may hold values from -3 to 3
- conv_x_bias: float32 [4096], P('tp'), may hold values from -1.8 to 1.8
- conv_bc_weight: float32 [4, 256], replicated, may hold values from -3 to 3
- conv_bc_bias: float32 [256], replicated, may hold values from -1.8 to 1.8
- dt_bias: float32 [64], P('tp'), may hold values from -11 to -2
- a_log: float32 [64], P('tp'), may hold values from 0 to 2.77
- skip: float32 [64], P('tp'), may hold values from 0.5 to 2
- norm_weight: float32 [4096], P('tp'), may hold values from 0.1 to 1.9
- w_out: float32 [4096, 2048], P('tp', 'seq'), may hold values from -0.09375 to 0.09375
- lengths: int32 [8], replicated, may hold values from 1 to 2048, 4096 in all
- request_group: int32 [16], replicated, may hold values from 0 to 15
Outputs:
- mixed: bfloat16 [4096, 2048], P(('seq', 'tp'))
- request_states: float32 [16, 64, 64, 128], P('seq', 'tp')
Inputs may be any that keep to these rules, and one draw needn't show every extreme that they name: 8 prompts packed end to end in this order; the lengths sum to 4096 and the longest is exactly 2048.
All inputs are finite; a program needn't handle non-finite values.
Results may differ from a plain program's by a relative error of at most 0.011.
Values may be sent and summed in bfloat16 or wider, within the bound.
No kernel may reach another device: no remote copies, remote signals or barrier semaphores. Data moves between devices by JAX's collectives and lax.ppermute only.
A program may use at most 128 MiB of HBM per device.

v0:
```python
import functools

import jax
import jax.numpy as jnp
from jax import lax
from jax.experimental import pallas as pl
from jax.experimental.pallas import tpu as pltpu
from jax.sharding import PartitionSpec as P

GROUP = 256
HALO = 16
LANES = 128
TERMS = 32
MM = jnp.bfloat16
F32 = jnp.float32
NEGATIVE = -1e30
sds = jax.ShapeDtypeStruct
VMEM_BYTES = 20 * 1024 * 1024

epsilon = 1e-05

ANY = pl.BlockSpec(memory_space=pl.ANY)
SMEM = pl.BlockSpec(memory_space=pltpu.SMEM)
VMEM = pl.BlockSpec(memory_space=pltpu.VMEM)


def flip(x, bits):
    count = lax.axis_size("seq")
    return lax.ppermute(x, "seq", [(i, i ^ bits) for i in range(count)])


def shift(x, by):
    count = lax.axis_size("tp")
    return lax.ppermute(x, "tp", [(i, (i + by) % count) for i in range(count)])


def plane_near(block):
    chips = lax.axis_size("seq") // 2
    return {k: (block if k == 0 else flip(block, 2 * k),) for k in range(chips) if k & (k - 1) == 0}


def plane_far(blocks):
    chips = lax.axis_size("seq") // 2
    blocks = dict(blocks)

    def half(k, side):
        if len(blocks[k]) == 2:
            return blocks[k][side]
        size = blocks[k][0].shape[0] // 2
        return blocks[k][0][side * size : (side + 1) * size]

    for k in range(1, chips):
        if k not in blocks:
            low = k & -k
            high = 1 << (k.bit_length() - 1)
            first = flip(half(k ^ low, 0), 2 * low)
            second = flip(half(k ^ high, 1), 2 * high)
            blocks[k] = (first, second)
    return blocks


def call(kernel, outs, in_specs, scratch=(), flops=0, moved=0, out_specs=None, name=None):
    return pl.pallas_call(
        kernel,
        out_shape=outs,
        in_specs=in_specs,
        out_specs=[VMEM] * len(outs) if out_specs is None else out_specs,
        scratch_shapes=list(scratch),
        compiler_params=pltpu.CompilerParams(vmem_limit_bytes=VMEM_BYTES),
        cost_estimate=pl.CostEstimate(flops=flops, bytes_accessed=moved, transcendentals=0),
        name=name,
    )


def split_terms(x):
    high = x.astype(MM).astype(F32)
    rest = x - high
    mid = rest.astype(MM).astype(F32)
    return high, mid, (rest - mid).astype(MM).astype(F32)


def silu(x):
    half = 0.5 * x
    return half + half * jnp.tanh(half)


def run_all(copies):
    for copy in copies:
        copy.start()
    for copy in copies:
        copy.wait()


def starts_of(position, ints):
    start, end = jnp.zeros_like(position), 0
    for i in range(ints.prompts):
        end = end + ints.ref[3 + i]
        start = jnp.where(position >= end, end, start)
    return start


class Ints:
    def __init__(self, ref, prompts):
        self.ref, self.prompts = ref, prompts
        self.t, self.p, self.c = ref[0], ref[1], ref[2]

    def wanted(self, i):
        return self.ref[3 + self.prompts + i]


def rows_at(first, size):
    return pl.ds(pl.multiple_of(first, 16), size)


def pack_x_kernel(tp_count, ints, w_ref, bc_ref, dt_ref, *outs):
    t = ints[0]
    pair = w_ref.shape[1] // tp_count
    inner = pair // 2
    bc_width = bc_ref.shape[1]
    heads = dt_ref.shape[1] // tp_count
    low_bc = bc_ref[...].astype(MM)
    for j, out in enumerate(outs):
        owner = lax.rem(t + j, tp_count)
        at = pl.multiple_of(owner * pair, LANES)
        out[:, :inner] = w_ref[:, pl.ds(at, inner)].astype(MM)
        out[:, inner : inner + bc_width] = low_bc
        steps = jnp.zeros((dt_ref.shape[0], heads), F32)
        for u in range(tp_count):
            steps = jnp.where(owner == u, dt_ref[:, u * heads : (u + 1) * heads], steps)
        steps = jnp.concatenate(
            [steps, jnp.zeros((dt_ref.shape[0], LANES - heads), F32)], axis=1
        )
        out[:, inner + bc_width : inner + bc_width + LANES] = steps.astype(MM)
        at = pl.multiple_of(owner * pair + inner, LANES)
        out[:, inner + bc_width + LANES :] = w_ref[:, pl.ds(at, inner)].astype(MM)


def pack_z_kernel(tp_count, ints, w_ref, *outs):
    pair = w_ref.shape[1] // tp_count
    for j, out in enumerate(outs):
        at = pl.multiple_of(lax.rem(ints[0] + j, tp_count) * pair, LANES)
        out[...] = w_ref[:, pl.ds(at, pair)].astype(MM)


def assemble_x_kernel(tp_count, ints, *refs):
    pieces, out = refs[:tp_count], refs[tp_count]
    rows = pieces[0].shape[0]
    for j, piece in enumerate(pieces):
        source = lax.rem(ints[0] + tp_count - j, tp_count)
        out[rows_at(source * rows, rows), :] = piece[...]


def assemble_z_kernel(tp_count, ints, *refs):
    pieces, (mine, theirs) = refs[:tp_count], refs[tp_count:]
    rows, inner = pieces[0].shape[0], mine.shape[1]
    c = ints[2]
    for j, piece in enumerate(pieces):
        at = rows_at(lax.rem(ints[0] + tp_count - j, tp_count) * rows, rows)
        mine[at, :] = piece[:, pl.ds(pl.multiple_of(c * inner, LANES), inner)]
        theirs[at, :] = piece[:, pl.ds(pl.multiple_of((1 - c) * inner, LANES), inner)]


def merge_kernel(ints, mine, theirs, out):
    rows = mine.shape[0]
    out[rows_at(ints[2] * rows, rows), :] = mine[...]
    out[rows_at((1 - ints[2]) * rows, rows), :] = theirs[...]


def lane_row(ref, first, count):
    lane = lax.broadcasted_iota(jnp.int32, (1, LANES), 1)
    row = jnp.zeros((1, LANES), F32)
    for i in range(count):
        row = jnp.where(lane == i, ref[first + i], row)
    return row


def front_kernel(sizes, ints_ref, floats, vecs, tok_ref, *refs):
    inner, bc_width, heads, prompts, where, depth, groups, side = sizes
    ints = Ints(ints_ref, prompts)
    c = ints.c
    conv = inner + bc_width
    state = bc_width // 2
    head_width = inner // heads
    half = groups // 2
    if where:
        pieces = refs[: len(where)]
        xs_ref, bc_ref, cum_ref, step_ref, message, weights, raw, sems = refs[len(where) :]
        start_x = pl.multiple_of(c * (conv + LANES), LANES)
        copies = []
        for piece, (k, other, first) in zip(pieces, where):
            core = 1 - c if other else c
            rows = rows_at(((ints.p ^ k) * 2 + core) * depth + first, piece.shape[0])
            for source, goal, size in ((start_x, 0, inner), (inner, inner, bc_width + LANES)):
                copies.append(
                    pltpu.make_async_copy(
                        piece.at[:, pl.ds(source, size)],
                        weights.at[rows, pl.ds(goal, size)],
                        sems.at[len(copies)],
                    )
                )
        run_all(copies)
    else:
        weights, xs_ref, bc_ref, cum_ref, step_ref, message, raw = refs
    taps = 4
    lower = (
        lax.broadcasted_iota(jnp.int32, (GROUP, GROUP), 0)
        >= lax.broadcasted_iota(jnp.int32, (GROUP, GROUP), 1)
    ).astype(F32)
    within = lax.broadcasted_iota(jnp.int32, (GROUP, LANES), 0)
    base = ints.p * (groups * GROUP) + side * half * GROUP
    all_heads = 2 * heads
    bias = lane_row(floats, c * heads, heads)
    rate = -jnp.exp(lane_row(floats, all_heads + c * heads, heads))

    def project(g):
        at = (side * half + g) * GROUP
        value = jnp.dot(
            tok_ref[at : at + GROUP + HALO, :], weights[...], preferred_element_type=F32
        )
        raw[g % 2, :, :conv] = value[:, :conv].astype(MM).astype(F32)
        raw[g % 2, :, conv:] = value[:, conv:]

    def one(g):
        rows = slice(g * GROUP, (g + 1) * GROUP)
        slot = g % 2
        first = base + g * GROUP
        position = first + within
        behind = position - starts_of(position, ints)
        keeps = [(behind >= lag).astype(F32) for lag in range(1, taps)]
        dt = raw[slot, HALO : HALO + GROUP, conv:]
        dt = jnp.where(c == 0, dt, pltpu.roll(dt, LANES - heads, 1)) + bias
        step = jnp.maximum(dt, 0.0) + jnp.log1p(jnp.exp(-jnp.abs(dt)))
        cum = jnp.dot(
            lower, step * rate, precision=lax.Precision.HIGHEST, preferred_element_type=F32
        )
        cum_ref[rows, :] = cum
        step_ref[rows, :] = step
        last = cum[GROUP - 1 : GROUP, :]
        start_last = starts_of(first + (GROUP - 1), ints)
        tail = jnp.where(position >= start_last, jnp.exp(last - cum), 0.0) * step
        for block in range(0, conv, LANES):
            lanes = slice(block, block + LANES)
            if block < inner:
                here = pl.ds(pl.multiple_of(c * inner + block, LANES), LANES)
                weight, offset = vecs[0:taps, here], vecs[taps : taps + 1, here]
            else:
                here = slice(block - inner, block - inner + LANES)
                weight, offset = vecs[8 : 8 + taps, here], vecs[8 + taps : 9 + taps, here]
            total = offset + raw[slot, HALO : HALO + GROUP, lanes] * weight[taps - 1 : taps]
            for lag in range(1, taps):
                term = raw[slot, HALO - lag : HALO - lag + GROUP, lanes] * keeps[lag - 1]
                total = total + term * weight[taps - 1 - lag : taps - lag]
            value = silu(total).astype(MM)
            if block < inner:
                xs_ref[rows, lanes] = value
            else:
                bc_ref[rows, here] = value
        b_wide = bc_ref[rows, :state].astype(F32)
        for h in range(0, heads, 2):
            weighted = jnp.concatenate(
                [(b_wide * tail[:, h + i : h + i + 1]).astype(MM) for i in range(2)], axis=1
            )
            both = lax.dot_general(
                xs_ref[rows, h * head_width : (h + 2) * head_width],
                weighted,
                (((0,), (0,)), ((), ())),
                preferred_element_type=F32,
            )
            at = h * head_width
            message[g, at : at + head_width, :] = both[:head_width, :state].astype(MM)
            at = at + head_width
            message[g, at : at + head_width, :] = both[head_width:, state:].astype(MM)
        spread = jnp.broadcast_to(jnp.exp(last), (8, LANES))
        diagonal = lax.broadcasted_iota(jnp.int32, (8, LANES), 0) == lax.broadcasted_iota(
            jnp.int32, (8, LANES), 1
        )
        gates = jnp.sum(jnp.where(diagonal, spread, 0.0), axis=1, keepdims=True)
        gates = jnp.where(start_last < first, jnp.broadcast_to(gates, (8, LANES)), 0.0)
        terms = jnp.concatenate(list(split_terms(gates)) + [jnp.zeros_like(gates)], axis=0)
        message[g, inner : inner + TERMS, :] = terms.astype(MM)

    project(0)
    for g in range(half):
        if g + 1 < half:
            project(g + 1)
        one(g)


def mid_kernel(sizes, ints_ref, floats, xs_ref, bc_ref, cum_ref, step_ref, y_ref, keep_ref):
    inner, heads, prompts, groups, side = sizes
    ints = Ints(ints_ref, prompts)
    state = bc_ref.shape[1] // 2
    head_width = inner // heads
    half = groups // 2
    base = ints.p * (groups * GROUP) + side * half * GROUP
    within_i = lax.broadcasted_iota(jnp.int32, (GROUP, GROUP), 0)
    within_j = lax.broadcasted_iota(jnp.int32, (GROUP, GROUP), 1)
    lane = lax.broadcasted_iota(jnp.int32, (GROUP, LANES), 1)
    skip_at = 4 * heads + ints.c * heads

    @pl.loop(0, half)
    def _(g):
        rows = rows_at(g * GROUP, GROUP)
        first = base + g * GROUP
        start = starts_of(first + within_i, ints)
        seen = (within_j <= within_i) & (first + within_j >= start)
        scores = lax.dot_general(
            bc_ref[rows, state:],
            bc_ref[rows, :state],
            (((1,), (1,)), ((), ())),
            preferred_element_type=F32,
        )
        cum = cum_ref[rows, :]
        cum_t = cum.T
        step_t = step_ref[rows, :].T
        keep = jnp.where(start[:, :LANES] < first, jnp.exp(cum), 0.0)
        for h in range(0, heads, 2):
            lanes = slice(h * head_width, (h + 2) * head_width)
            pair = xs_ref[rows, lanes]
            first_skip, second_skip = (floats[skip_at + h + i] for i in range(2))
            total = jnp.where(lane < head_width, first_skip, second_skip) * pair.astype(F32)
            for i in range(2):
                log_decay = cum[:, h + i : h + i + 1] - cum_t[h + i : h + i + 1, :]
                decay = jnp.exp(jnp.where(seen, log_decay, NEGATIVE))
                mix = (decay * scores * step_t[h + i : h + i + 1, :]).astype(MM)
                own = jnp.where((lane < head_width) == (i == 0), pair, jnp.zeros_like(pair))
                total = total + jnp.dot(mix, own, preferred_element_type=F32)
            y_ref[rows, lanes] = total
            keep_ref[rows, lanes] = jnp.where(
                lane < head_width, keep[:, h : h + 1], keep[:, h + 1 : h + 2]
            )


def gate_kernel(sizes, ints, tok_ref, *refs):
    inner, where, depth = sizes
    pieces = refs[: len(where)]
    low, high, weights, sems = refs[len(where) :]
    copies = []
    for i, (piece, (k, first)) in enumerate(zip(pieces, where)):
        rows = rows_at((ints[1] ^ k) * depth + first, piece.shape[0])
        copies.append(pltpu.make_async_copy(piece, weights.at[rows, :], sems.at[i]))
    run_all(copies)
    count = low.shape[0] // GROUP
    for side, out in enumerate((low, high)):

        @pl.loop(0, count)
        def _(g):
            row = (side * count + g) * GROUP + HALO
            value = jnp.dot(
                tok_ref[rows_at(row, GROUP), :], weights[...], preferred_element_type=F32
            )
            out[rows_at(g * GROUP, GROUP), :] = silu(value.astype(MM).astype(F32))


def gating(sizes, ints, low_states, vecs, side, y_ref, keep_ref, gate_ref, bc_ref, out):
    inner, heads, groups = sizes
    half = groups // 2
    state = bc_ref.shape[1] // 2
    lane = lax.broadcasted_iota(jnp.int32, (GROUP, LANES), 1)
    for g in range(half):
        rows = slice(g * GROUP, (g + 1) * GROUP)
        carried = lax.dot_general(
            bc_ref[rows, state:],
            low_states[side * half + g],
            (((1,), (1,)), ((), ())),
            preferred_element_type=F32,
        )
        squares = jnp.zeros((GROUP, LANES), F32)
        for at in range(0, inner, LANES):
            lanes = slice(at, at + LANES)
            y = y_ref[rows, lanes] + carried[:, lanes] * keep_ref[rows, lanes]
            gated = y * gate_ref[rows, lanes]
            squares = squares + gated * gated
            here = pl.ds(pl.multiple_of(ints[2] * inner + at, LANES), LANES)
            out[rows, lanes] = (gated * vecs[5:6, here]).astype(MM)
        total = jnp.broadcast_to(jnp.sum(squares, axis=1, keepdims=True), (GROUP, LANES))
        out[rows, inner:] = spread_terms(total).astype(MM)


def spread_terms(total):
    lane = lax.broadcasted_iota(jnp.int32, total.shape, 1)
    high, mid, low = split_terms(total)
    return jnp.where(lane == 0, high, jnp.where(lane == 1, mid, jnp.where(lane == 2, low, 0.0)))


def added_terms(ref, at):
    value = ref[:, at:].astype(F32)
    return jnp.broadcast_to(jnp.sum(value, axis=1, keepdims=True), value.shape)


def back_kernel(sizes, ints_ref, vecs, *refs):
    inner, heads, prompts, groups, n_pieces, per = sizes
    pieces = refs[:n_pieces]
    sides = (refs[n_pieces : n_pieces + 4], refs[n_pieces + 4 : n_pieces + 8])
    theirs, low_states, asked, own_asked, parts, states, sems = refs[n_pieces + 8 :]
    ints = Ints(ints_ref, prompts)
    p, c = ints.p, ints.c
    head_width = inner // heads
    half = groups // 2
    copies = []
    for i, piece in enumerate(pieces):
        k, side = i // 2, i % 2
        at = (p ^ k) * groups + side * half
        copies.append(pltpu.make_async_copy(piece, parts.at[pl.ds(at, half)], sems.at[i]))
    run_all(copies)
    blocks = parts.shape[0]
    states[0] = jnp.zeros(states.shape[1:], F32)

    @pl.loop(0, blocks)
    def _(b):
        terms = parts[b, inner : inner + TERMS, :].astype(F32)
        gates = terms[0:8] + terms[8:16] + terms[16:24]
        for h in range(heads):
            rows = slice(h * head_width, (h + 1) * head_width)
            states[b + 1, rows, :] = gates[h : h + 1, :] * states[b, rows, :] + parts[
                b, rows, :
            ].astype(F32)

    for g in range(groups):
        low_states[g] = states[p * groups + g].astype(MM)
    for side in range(2):

        @pl.when(c != side)
        def _():
            gating((inner, heads, groups), ints_ref, low_states, vecs, side, *sides[side], theirs)

    for i in range(per):
        own_asked[i] = states[ints.wanted((p * 2 + c) * per + i) + 1]
        asked[i] = states[ints.wanted((p * 2 + 1 - c) * per + i) + 1].astype(MM)


def back_own_kernel(sizes, ints_ref, vecs, low_states, *refs):
    sides = (refs[:4], refs[4:8])
    mine = refs[8]
    for side in range(2):

        @pl.when(ints_ref[2] == side)
        def _():
            gating(sizes, ints_ref, low_states, vecs, side, *sides[side], mine)


def block_places(t, tp_count):
    if tp_count == 4:
        return [jnp.where(t < 2, 3, 0), jnp.where(t < 2, 2, 1), t ^ 1, t]
    return [lax.rem(t + j, tp_count) for j in range(1, tp_count)] + [t]


def out_kernel(sizes, ints, mine, theirs, *refs):
    inner, tp_count, chosen, where = sizes
    t, p, c = ints[0], ints[1], ints[2]
    if where:
        pieces = refs[: len(where)]
        outs = refs[len(where) : len(where) + len(chosen)]
        weights, sems = refs[len(where) + len(chosen) :]
        copies = []
        for i, (piece, (k, other, first)) in enumerate(zip(pieces, where)):
            rows, columns = piece.shape
            core = 1 - c if other else c
            at = pl.multiple_of(((p ^ k) * 2 + core) * columns, LANES)
            copies.append(
                pltpu.make_async_copy(
                    piece, weights.at[pl.ds(first, rows), pl.ds(at, columns)], sems.at[i]
                )
            )
        run_all(copies)
    else:
        weights, outs = refs[0], refs[1:]
    width = weights.shape[1]
    piece_rows = mine.shape[0] // tp_count
    own_rows = rows_at(c * inner, inner)
    other_rows = rows_at((1 - c) * inner, inner)
    for i, out in zip(chosen, outs):
        rows = rows_at(block_places(t, tp_count)[i] * piece_rows, piece_rows)
        sums = jnp.sum(
            mine[rows, inner:].astype(F32) + theirs[rows, inner:].astype(F32), axis=1, keepdims=True
        )
        out[:, width:] = spread_terms(jnp.broadcast_to(sums, (piece_rows, LANES))).astype(out.dtype)
        for at in range(0, width, 512):
            lanes = slice(at, at + 512)
            value = jnp.dot(mine[rows, :inner], weights[own_rows, lanes], preferred_element_type=F32)
            value = value + jnp.dot(
                theirs[rows, :inner], weights[other_rows, lanes], preferred_element_type=F32
            )
            out[:, lanes] = value.astype(out.dtype)


def add_kernel(got, own, out):
    width = out.shape[1] - LANES
    for at in range(0, width, 512):
        lanes = slice(at, at + 512)
        out[:, lanes] = (got[:, lanes].astype(F32) + own[:, lanes].astype(F32)).astype(MM)
    out[:, width:] = spread_terms(added_terms(got, width) + added_terms(own, width)).astype(MM)


def final_kernel(channels, own, *refs):
    received, out = refs[:-1], refs[-1]
    width = out.shape[1]
    squares = added_terms(own, width)
    for got in received:
        squares = squares + added_terms(got, width)
    factor = lax.rsqrt(squares[:, :1] / channels + epsilon)
    for at in range(0, width, 512):
        lanes = slice(at, at + 512)
        total = own[:, lanes]
        for got in received:
            total = total + got[:, lanes].astype(F32)
        out[:, lanes] = (total * factor).astype(out.dtype)


def sum_over_tp(blocks, own):
    tp_count = lax.axis_size("tp")
    if tp_count != 4:
        return own, [shift(x, j + 1) for j, x in enumerate(blocks)]

    def send(x, pairs):
        return lax.ppermute(x, "tp", pairs)

    def add(got, x, name):
        return call(add_kernel, [sds(x.shape, MM)], [VMEM] * 2, moved=1_700_000, name=name)(got, x)[0]

    far, mid, near = blocks
    far_got = send(far, [(0, 1), (3, 2)])
    to_end = send(near, [(1, 0), (2, 3)])
    far_got, mid, near, own = lax.optimization_barrier((far_got, mid, near, own))
    mid_got = send(mid, [(0, 1), (3, 2)])
    far_sum = send(add(far_got, far, "add_far"), [(1, 3), (2, 0)])
    mid_got, near = lax.optimization_barrier((mid_got, near))
    to_inner = send(near, [(0, 1), (3, 2)])
    mid_sum = send(add(mid_got, mid, "add_mid"), [(1, 2), (2, 1)])
    return own, [to_end, to_inner, far_sum, mid_sum]


def on_device(
    tokens,
    w_zx,
    w_dt,
    w_bc,
    conv_x_weight,
    conv_x_bias,
    conv_bc_weight,
    conv_bc_bias,
    dt_bias,
    a_log,
    skip,
    norm_weight,
    w_out,
    lengths,
    request_group,
):
    tp_count, seq_count = lax.axis_size("tp"), lax.axis_size("seq")
    t, s = lax.axis_index("tp"), lax.axis_index("seq")
    chips = seq_count // 2
    p, c = s // 2, s % 2
    tok_dev, width = tokens.shape
    rows = w_zx.shape[0]
    inner_all = w_zx.shape[1] // 2
    pair = conv_x_weight.shape[1]
    inner = pair // 2
    heads = dt_bias.shape[0] // 2
    head_width = inner // heads
    bc_width = w_bc.shape[1]
    state = bc_width // 2
    tok = 2 * tok_dev
    groups = tok // GROUP
    half = groups // 2
    conv = inner + bc_width
    prompts = lengths.shape[0]
    x_width = 2 * inner + bc_width + LANES
    depth = tp_count * rows

    ints = jnp.concatenate([jnp.stack([t, p, c]).astype(jnp.int32), lengths, request_group])
    floats = jnp.concatenate([dt_bias, a_log, skip])
    vecs = jnp.concatenate(
        [
            conv_x_weight,
            conv_x_bias[None, :],
            norm_weight[None, :],
            jnp.zeros((2, pair), F32),
            jnp.pad(conv_bc_weight, ((0, 0), (0, pair - bc_width))),
            jnp.pad(conv_bc_bias[None, :], ((0, 3), (0, pair - bc_width))),
        ],
        axis=0,
    )

    def packed(kernel, operands, specs, wide, name):
        return pl.pallas_call(
            functools.partial(kernel, tp_count),
            grid=(1,),
            out_shape=[sds((rows, wide), MM)] * tp_count,
            in_specs=specs,
            out_specs=[pl.BlockSpec((rows, wide), lambda i: (0, 0))] * tp_count,
            compiler_params=pltpu.CompilerParams(vmem_limit_bytes=VMEM_BYTES),
            name=name,
        )(*operands)

    def whole(x):
        return pl.BlockSpec(x.shape, lambda i: (0, 0))

    def sent_over_tp(pieces):
        return [pieces[0]] + [shift(x, j) for j, x in enumerate(pieces) if j]

    def assembled(kernel, outs, pieces, name):
        return call(
            functools.partial(kernel, tp_count), outs, [SMEM] + [VMEM] * tp_count, name=name
        )(ints, *pieces)

    def together(*lists):
        joined = lax.optimization_barrier(tuple(tuple(one) for one in lists))
        return [list(one) for one in joined]

    x_sent = packed(
        pack_x_kernel,
        (ints, w_zx, w_bc, w_dt),
        [SMEM, pl.BlockSpec((rows, inner_all), lambda i: (0, 1)), whole(w_bc), whole(w_dt)],
        x_width,
        "pack_x",
    )
    x_got = sent_over_tp(x_sent)

    out_near = plane_near(w_out.astype(MM))
    keys = list(out_near)
    x_got[1:2], out_got = together(x_got[1:2], [out_near[k][0] for k in keys])
    out_blocks = plane_far({k: (piece,) for k, piece in zip(keys, out_got)})
    out_own = [piece for k in out_blocks for piece in out_blocks[k]]
    out_where = [
        (k, 0, i * (w_out.shape[0] // 2)) for k in out_blocks for i in range(len(out_blocks[k]))
    ]
    (x_block,) = assembled(assemble_x_kernel, [sds((depth, x_width), MM)], x_got, "assemble_x")

    other = flip(tokens, 1)
    first_tok = jnp.where(c == 0, tokens, other)
    second_tok = jnp.where(c == 0, other, tokens)
    before = lax.ppermute(
        second_tok[tok_dev - HALO :], "seq", [(i, i + 2) for i in range(seq_count - 2)]
    )
    all_tok = jnp.concatenate([before, first_tok, second_tok], axis=0)

    (x_block, all_tok, ints, floats, vecs), out_own = together(
        [x_block, all_tok, ints, floats, vecs], out_own
    )
    near = plane_near(x_block)
    z_sent = packed(
        pack_z_kernel,
        (ints, w_zx),
        [SMEM, pl.BlockSpec((rows, inner_all), lambda i: (0, 0))],
        2 * inner,
        "pack_z",
    )
    z_got = sent_over_tp(z_sent)
    own_other = flip(x_block, 1)
    blocks, z_got = together([near[k][0] for k in near if k], z_got)
    far = plane_far({k: (block,) for k, block in zip(near, [x_block] + blocks)})
    where = [(k, 0, i * depth // 2) for k in far for i in range(len(far[k]))]
    x_pieces = [piece for k in far for piece in far[k]]
    x_pieces += [own_other] + [flip(piece, 1) for piece in x_pieces[1:]]
    where = tuple(where + [(k, 1, first) for k, _, first in where])
    z_mine, z_theirs = assembled(
        assemble_z_kernel, [sds((depth, inner), MM)] * 2, z_got, "assemble_z"
    )
    (z_block,) = call(
        merge_kernel, [sds((2 * depth, inner), MM)], [SMEM, VMEM, VMEM], name="merge_z"
    )(ints, z_mine, flip(z_theirs, 1))
    x_pieces, (z_block,) = together(x_pieces, [z_block])

    def front(side, where, operands):
        outs = [
            sds((tok_dev, inner), MM),
            sds((tok_dev, bc_width), MM),
            sds((tok_dev, LANES), F32),
            sds((tok_dev, LANES), F32),
            sds((half, inner + TERMS, state), MM),
        ]
        scratch = [pltpu.VMEM((2, HALO + GROUP, conv + LANES), F32)]
        if where:
            outs.append(sds((width, conv + LANES), MM))
            scratch.append(pltpu.SemaphoreType.DMA((2 * len(where),)))
        return call(
            functools.partial(
                front_kernel, (inner, bc_width, heads, prompts, where, depth, groups, side)
            ),
            outs,
            [SMEM, SMEM, VMEM, VMEM] + ([ANY] * len(where) if where else [VMEM]),
            scratch,
            flops=2 * (tok_dev + HALO) * width * (conv + LANES),
            moved=8_000_000,
            name="front_%d" % side,
        )(ints, floats, vecs, all_tok, *operands)

    z_near = plane_near(z_block)
    *first, weights = front(0, where, x_pieces)
    *first, weights = together([*first, weights])[0]

    low_near = plane_near(first[4])
    out_other = [flip(piece, 1) for piece in out_own]
    out_where = tuple(out_where + [(k, 1, first_row) for k, _, first_row in out_where])
    second = front(1, (), [weights])
    second, lows, z_blocks, out_other = together(
        second,
        [low_near[k][0] for k in low_near],
        [z_near[k][0] for k in z_near],
        out_other,
    )
    out_pieces = out_own + out_other
    z_far = plane_far({k: (block,) for k, block in zip(z_near, z_blocks)})
    z_where = tuple((k, i * depth) for k in z_far for i in range(len(z_far[k])))
    z_pieces = [piece for k in z_far for piece in z_far[k]]

    def mid(side, xs, bc, cum, step, message):
        return call(
            functools.partial(mid_kernel, (inner, heads, prompts, groups, side)),
            [sds((tok_dev, inner), F32)] * 2,
            [SMEM, SMEM] + [VMEM] * 4,
            flops=2 * tok_dev * GROUP * inner,
            moved=1_000_000,
            name="mid_%d" % side,
        )(ints, floats, xs, bc, cum, step)

    parts = {k: (block, None) for k, block in zip(low_near, lows)}
    high_near = plane_near(second[4])
    first_y = mid(0, *first)
    highs, first_y = together([high_near[k][0] for k in parts], first_y)
    parts = {k: (parts[k][0], high) for k, high in zip(parts, highs)}
    for k in range(1, chips):
        if k not in parts:
            low, high = k & -k, 1 << (k.bit_length() - 1)
            parts[k] = (flip(parts[k ^ low][0], 2 * low), flip(parts[k ^ high][1], 2 * high))
    parts = [piece for k in range(chips) for piece in parts[k]]

    y = [first_y, mid(1, *second)]
    gate = call(
        functools.partial(gate_kernel, (inner, z_where, 2 * depth)),
        [sds((tok_dev, inner), F32)] * 2,
        [SMEM, VMEM] + [ANY] * len(z_where),
        [pltpu.VMEM((width, inner), MM), pltpu.SemaphoreType.DMA((len(z_where),))],
        flops=tok * width * inner // 4,
        moved=1_000_000,
        name="gate",
    )(ints, all_tok, *z_pieces)
    sides = [*y[0], gate[0], first[1], *y[1], gate[1], second[1]]
    parts, sides = together(parts, sides)

    per = request_group.shape[0] // seq_count
    sent = sds((tok_dev, inner + LANES), MM)
    theirs, low_states, asked, own_asked = call(
        functools.partial(back_kernel, (inner, heads, prompts, groups, len(parts), per)),
        [
            sent,
            sds((groups, inner, state), MM),
            sds((per, inner, state), MM),
            sds((per, inner, state), F32),
        ],
        [SMEM, VMEM] + [ANY] * len(parts) + [VMEM] * 8,
        [
            pltpu.VMEM((chips * groups, inner + TERMS, state), MM),
            pltpu.VMEM((chips * groups + 1, inner, state), F32),
            pltpu.SemaphoreType.DMA((len(parts),)),
        ],
        flops=2 * tok * state * inner,
        moved=8_000_000,
        name="back",
    )(ints, vecs, *parts, *sides)
    theirs = flip(theirs, 1)
    (mine,) = call(
        functools.partial(back_own_kernel, (inner, heads, groups)),
        [sent],
        [SMEM] + [VMEM] * 10,
        flops=2 * tok_dev * state * inner,
        moved=4_000_000,
        name="back_own",
    )(ints, vecs, low_states, *sides)

    out_width = seq_count * w_out.shape[1]
    piece = tok_dev // tp_count
    block = sds((piece, out_width + LANES), MM)
    ahead = tp_count - 2

    def project_out(chosen, outs, where, operands):
        scratch, extra = [], []
        if where:
            extra = [sds((2 * inner, out_width), MM)]
            scratch = [pltpu.SemaphoreType.DMA((len(where),))]
        return call(
            functools.partial(out_kernel, (inner, tp_count, chosen, where)),
            outs + extra,
            [SMEM, VMEM, VMEM] + ([ANY] * len(where) if where else [VMEM]),
            scratch,
            flops=4 * len(outs) * piece * inner * out_width,
            moved=8_000_000,
            name="out_%d" % len(chosen),
        )(ints, mine, theirs, *operands)

    *sent_first, out_weights = project_out(
        tuple(range(ahead)), [block] * ahead, out_where, out_pieces
    )
    near_block, own = project_out(
        (ahead, ahead + 1), [block, sds(block.shape, F32)], (), [out_weights]
    )
    own, received = sum_over_tp([*sent_first, near_block], own)
    (mixed,) = call(
        functools.partial(final_kernel, float(inner_all)),
        [sds((piece, out_width), MM)],
        [VMEM] * (1 + len(received)),
        name="final",
    )(own, *received)

    other_asked = flip(asked, 1).astype(F32)
    states = jnp.where(
        c == 0,
        jnp.concatenate([own_asked, other_asked], axis=1),
        jnp.concatenate([other_asked, own_asked], axis=1),
    )
    return (mixed, states.reshape(per, 2 * heads, head_width, state))


def solution(mesh):
    return jax.shard_map(
        on_device,
        mesh=mesh,
        in_specs=(
            P("seq", None),
            P(("seq", "tp"), None),
            P(("seq", "tp"), None),
            P(("seq", "tp"), None),
            P(None, "tp"),
            P("tp"),
            P(),
            P(),
            P("tp"),
            P("tp"),
            P("tp"),
            P("tp"),
            P("tp", "seq"),
            P(),
            P(),
        ),
        out_specs=(P(("seq", "tp"), None), P("seq", "tp", None, None)),
        check_vma=False,
    )
```

profile of v0, /device:TPU:0, one launch (start us, length us, event | category | flops | bytes accessed | tf_op | source)
XLA Modules:
  0.0 171.8 jit_solution(17759821387332984587)
XLA Ops:
  1.2 1.3 convert_element_type.10.refs_0_
  2.5 2.6 %collective-permute-start.1 = (bf16[1024,256]{1,0:T(8,128)(2,1)S(1)}, bf16[1024,256]{1,0:T(8,128)(2,1)S(1)}, u32[]{:S(2)}, u32[]{:S(2)}) collective-permute-start(bf16[1024,256]{1,0:T(8,128)(2,1)S(1)} %convert_element_type.10.refs_0_), channel_id=1, source_target_pairs={{0,8},{4,12},{8,0},{12,4},{16,24},{20,28},{24,16},{28,20},{1,9},{5... | collective-permute-start | bytes 1572872 | tf_op jit(solution)/shard_map/ppermute | solution.py:29
  5.0 1.5 collective-permute-start.2
  6.6 0.7 concatenate.18.ints.ints_ref
  7.3 1.6 copy-done
  8.9 0.8 copy-done.2
  9.8 0.8 copy-done.3
  10.5 0.9 pack_x.1
  11.4 1.6 collective-permute-start
  13.0 2.6 %collective-permute-start.3 = (bf16[64,1408]{1,0:T(8,128)(2,1)S(1)}, bf16[64,1408]{1,0:T(8,128)(2,1)S(1)}, u32[]{:S(2)}, u32[]{:S(2)}) collective-permute-start(bf16[64,1408]{1,0:T(8,128)(2,1)S(1)} %get-tuple-element.115), channel_id=1, source_target_pairs={{0,2},{1,3},{2,0},{3,1},{4,6},{5,7},{6,4},{7,5},{8,10},{9,11},{10,... | collective-permute-start | bytes 540680 | tf_op jit(solution)/shard_map/ppermute | solution.py:34
  15.8 1.4 collective-permute-start.4
  17.2 2.5 %broadcast_select_fusion = (bf16[512,2048]{1,0:T(8,128)(2,1)S(1)}, bf16[512,2048]{1,0:T(8,128)(2,1)S(1)}) fusion(bf16[512,2048]{1,0:T(8,128)(2,1)} %param.15, bf16[512,2048]{1,0:T(8,128)(2,1)} %collective-permute-done.5, pred[]{:T(512)S(6)} %eq.4), kind=kLoop, calls=%fused_computation.1 | loop fusion | flops 2097152 | bytes 8388609 | tf_op jit(solution)/shard_map/jit(_where)/select_n | solution.py:631
  19.7 1.1 collective-permute-done.refs_1_
  20.7 2.4 %collective-permute-start.6 = (bf16[16,2048]{1,0:T(8,128)(2,1)S(1)}, bf16[16,2048]{1,0:T(8,128)(2,1)S(1)}, u32[]{:S(2)}, u32[]{:S(2)}) collective-permute-start(bf16[16,2048]{1,0:T(8,128)(2,1)S(1)} %slice.28), channel_id=1, source_target_pairs={{0,8},{4,12},{8,16},{12,20},{16,24},{20,28},{1,9},{5,13},{9,17},{1... | collective-permute-start | bytes 196616 | tf_op jit(solution)/shard_map/ppermute | solution.py:633
  23.3 1.5 collective-permute-start.7
  24.9 2.6 %collective-permute-done.3.refs_2_ = bf16[64,1408]{1,0:T(8,128)(2,1)S(1)} collective-permute-done((bf16[64,1408]{1,0:T(8,128)(2,1)S(1)}, bf16[64,1408]{1,0:T(8,128)(2,1)S(1)}, u32[]{:S(2)}, u32[]{:S(2)}) %collective-permute-start.3) | collective-permute-done | bytes 180256 | tf_op jit(solution)/shard_map/ppermute | solution.py:34
  28.5 1.8 %collective-permute-done.7.refs_3_ = bf16[512,256]{1,0:T(8,128)(2,1)S(1)} collective-permute-done((bf16[512,256]{1,0:T(8,128)(2,1)S(1)}, bf16[512,256]{1,0:T(8,128)(2,1)S(1)}, u32[]{:S(2)}, u32[]{:S(2)}) %collective-permute-start.7) | collective-permute-done | bytes 262176 | tf_op jit(solution)/shard_map/ppermute | solution.py:29
  30.3 1.0 collective-permute-done.8.refs_4_
  32.7 9.2 %collective-permute-start.11 = (bf16[64,1024]{1,0:T(8,128)(2,1)S(1)}, bf16[64,1024]{1,0:T(8,128)(2,1)S(1)}, u32[]{:S(2)}, u32[]{:S(2)}) collective-permute-start(bf16[64,1024]{1,0:T(8,128)(2,1)S(1)} %get-tuple-element.126), channel_id=1, source_target_pairs={{0,1},{1,2},{2,3},{3,0},{4,5},{5,6},{6,7},{7,4},{8,9},{9,10},{10,1... | collective-permute-start | bytes 393224 | tf_op jit(solution)/shard_map/ppermute | solution.py:34
  41.9 2.6 %collective-permute-start.12 = (bf16[64,1024]{1,0:T(8,128)(2,1)S(1)}, bf16[64,1024]{1,0:T(8,128)(2,1)S(1)}, u32[]{:S(2)}, u32[]{:S(2)}) collective-permute-start(bf16[64,1024]{1,0:T(8,128)(2,1)S(1)} %get-tuple-element.127), channel_id=1, source_target_pairs={{0,2},{1,3},{2,0},{3,1},{4,6},{5,7},{6,4},{7,5},{8,10},{9,11},{10,... | collective-permute-start | bytes 393224 | tf_op jit(solution)/shard_map/ppermute | solution.py:34
  44.5 4.5 %collective-permute-start.13 = (bf16[64,1024]{1,0:T(8,128)(2,1)S(1)}, bf16[64,1024]{1,0:T(8,128)(2,1)S(1)}, u32[]{:S(2)}, u32[]{:S(2)}) collective-permute-start(bf16[64,1024]{1,0:T(8,128)(2,1)S(1)} %get-tuple-element.128), channel_id=1, source_target_pairs={{0,3},{1,0},{2,1},{3,2},{4,7},{5,4},{6,5},{7,6},{8,11},{9,8},{10,9... | collective-permute-start | bytes 393224 | tf_op jit(solution)/shard_map/ppermute | solution.py:34
  49.0 2.9 %collective-permute-done.12.refs_2_ = bf16[64,1024]{1,0:T(8,128)(2,1)S(1)} collective-permute-done((bf16[64,1024]{1,0:T(8,128)(2,1)S(1)}, bf16[64,1024]{1,0:T(8,128)(2,1)S(1)}, u32[]{:S(2)}, u32[]{:S(2)}) %collective-permute-start.12) | collective-permute-done | bytes 131104 | tf_op jit(solution)/shard_map/ppermute | solution.py:34
  51.9 5.3 %collective-permute-done.13.refs_3_ = bf16[64,1024]{1,0:T(8,128)(2,1)S(1)} collective-permute-done((bf16[64,1024]{1,0:T(8,128)(2,1)S(1)}, bf16[64,1024]{1,0:T(8,128)(2,1)S(1)}, u32[]{:S(2)}, u32[]{:S(2)}) %collective-permute-start.13) | collective-permute-done | bytes 131104 | tf_op jit(solution)/shard_map/ppermute | solution.py:34
  57.2 1.2 collective-permute-start.14
  58.4 1.9 %collective-permute-start.15 = (bf16[128,1408]{1,0:T(8,128)(2,1)S(1)}, bf16[128,1408]{1,0:T(8,128)(2,1)S(1)}, u32[]{:S(2)}, u32[]{:S(2)}) collective-permute-start(bf16[128,1408]{1,0:T(8,128)(2,1)S(1)} %slice.25), channel_id=1, source_target_pairs={{0,16},{4,20},{8,24},{12,28},{16,0},{20,4},{24,8},{28,12},{1,17},{... | collective-permute-start | bytes 1081352 | tf_op jit(solution)/shard_map/ppermute | solution.py:29
  60.8 3.9 %collective-permute-done.14.refs_3_ = bf16[128,1408]{1,0:T(8,128)(2,1)S(1)} collective-permute-done((bf16[128,1408]{1,0:T(8,128)(2,1)S(1)}, bf16[128,1408]{1,0:T(8,128)(2,1)S(1)}, u32[]{:S(2)}, u32[]{:S(2)}) %collective-permute-start.14) | collective-permute-done | bytes 360480 | tf_op jit(solution)/shard_map/ppermute | solution.py:29
  64.7 1.2 collective-permute-done.15.refs_4_
  67.1 1.2 collective-permute-done.21.theirs
  70.3 1.0 collective-permute-done.29.refs_8_
  71.3 0.9 collective-permute-start.24
  72.2 1.5 collective-permute-start.25
  73.8 6.5 %front_0.1 = (bf16[512,512]{1,0:T(8,128)(2,1)S(1)}, bf16[512,256]{1,0:T(8,128)(2,1)S(1)}, f32[512,128]{1,0:T(8,128)S(1)}, f32[512,128]{1,0:T(8,128)S(1)}, bf16[2...) custom-call(s32[27]{0:T(128)S(1)} %concatenate.18.ints.ints_ref, f32[48]{0:T(128)S(1)} %pad_maximum_fusion.1.floats, ...), custom_call_target="tpu_custom_call" | custom-call | flops 1937768448 | bytes 8000000 | tf_op jit(solution)/shard_map/front_0/pallas_call | solution.py:677
  80.2 1.5 collective-permute-start.22
  81.9 5.7 %front_1.1 = (bf16[512,512]{1,0:T(8,128)(2,1)S(1)}, bf16[512,256]{1,0:T(8,128)(2,1)S(1)}, f32[512,128]{1,0:T(8,128)S(1)}, f32[512,128]{1,0:T(8,128)S(1)}, bf16[2,544,128]{2,1,0:T(8,128)(2,1)S(1)}) custom-call(s32[27]{0:T(128)S(1)} %concatenate.18.ints.ints_ref, f32[48]{0:T(128)S(1)} %pad_maximum_fusion.1.floats, f32[16,1024]{1,0:T(8,128)S(1)} %concatenate.21.vecs, ...), custom_call_target="tpu_custom_call" | custom-call | flops 1937768448 | bytes 8000000 | tf_op jit(solution)/shard_map/front_1/pallas_call | solution.py:677
  87.6 3.9 %collective-permute-done.22.refs_2_ = bf16[2,544,128]{2,1,0:T(8,128)(2,1)S(1)} collective-permute-done((bf16[2,544,128]{2,1,0:T(8,128)(2,1)S(1)}, bf16[2,544,128]{2,1,0:T(8,128)(2,1)S(1)}, u32[]{:S(2)}, u32[]{:S(2)}) %collective-permute-start.22) | collective-permute-done | bytes 278560 | tf_op jit(solution)/shard_map/ppermute | solution.py:29
  92.1 1.2 collective-permute-start.31
  93.3 1.7 %collective-permute-start.32 = (bf16[2,544,128]{2,1,0:T(8,128)(2,1)S(1)}, bf16[2,544,128]{2,1,0:T(8,128)(2,1)S(1)}, u32[]{:S(2)}, u32[]{:S(2)}) collective-permute-start(bf16[2,544,128]{2,1,0:T(8,128)(2,1)S(1)} %get-tuple-element.187.refs_1_), channel_id=1, source_target_pairs={{0,16},{4,20},{8,24},{12,28},{16,0},{20,4},{24,8},{28,12},{1,17},{... | collective-permute-start | bytes 835592 | tf_op jit(solution)/shard_map/ppermute | solution.py:29
  95.1 0.7 collective-permute-start.35
  96.3 2.4 %mid_0.1 = (f32[512,512]{1,0:T(8,128)S(1)}, f32[512,512]{1,0:T(8,128)S(1)}) custom-call(s32[27]{0:T(128)S(1)} %concatenate.18.ints.ints_ref, f32[48]{0:T(128)S(1)} %pad_maximum_fusion.1.floats, bf16[512,512]{1,0:T(8,128)(2,1)S(1)} %get-tuple-element.162.xs_ref, bf16[512,256]{1,0:T(8,128)(2,1)S(1)} %get-tuple-element.197.bc_ref.refs_11_.refs_3_, ...), custom_call_target="tpu_custom_call" | custom-call | flops 134217728 | bytes 1000000 | tf_op jit(solution)/shard_map/mid_0/pallas_call | solution.py:709
  98.8 1.3 collective-permute-start.33
  100.1 1.6 collective-permute-done.31.refs_3_
  101.7 1.2 collective-permute-done.32.refs_5_
  102.9 1.7 %collective-permute-start.34 = (bf16[2,544,128]{2,1,0:T(8,128)(2,1)S(1)}, bf16[2,544,128]{2,1,0:T(8,128)(2,1)S(1)}, u32[]{:S(2)}, u32[]{:S(2)}) collective-permute-start(bf16[2,544,128]{2,1,0:T(8,128)(2,1)S(1)} %collective-permute-done.31.refs_3_), channel_id=1, source_target_pairs={{0,16},{4,20},{8,24},{12,28},{16,0},{20,4},{24,8},{28,12},{1,17},{... | collective-permute-start | bytes 835592 | tf_op jit(solution)/shard_map/ppermute | solution.py:29
  104.7 2.4 %mid_1.1 = (f32[512,512]{1,0:T(8,128)S(1)}, f32[512,512]{1,0:T(8,128)S(1)}) custom-call(s32[27]{0:T(128)S(1)} %concatenate.18.ints.ints_ref, f32[48]{0:T(128)S(1)} %pad_maximum_fusion.1.floats, bf16[512,512]{1,0:T(8,128)(2,1)S(1)} %get-tuple-element.179.xs_ref, bf16[512,256]{1,0:T(8,128)(2,1)S(1)} %get-tuple-element.201.bc_ref.refs_15_.refs_7_, ...), custom_call_target="tpu_custom_call" | custom-call | flops 134217728 | bytes 1000000 | tf_op jit(solution)/shard_map/mid_1/pallas_call | solution.py:709
  107.3 1.2 collective-permute-done.36.refs_4_
  108.5 4.0 %gate.1 = (f32[512,512]{1,0:T(8,128)S(1)}, f32[512,512]{1,0:T(8,128)S(1)}) custom-call(s32[27]{0:T(128)S(1)} %concatenate.18.ints.ints_ref, bf16[1040,2048]{1,0:T(8,128)(2,1)S(1)} %pad_maximum_fusion.tok_ref, bf16[512,512]{1,0:T(8,128)(2,1)S(1)} %merge_z.1.refs_0_, bf16[512,512]{1,0:T(8,128)(2,1)S(1)} %collective-permute-done.24.refs_1_, ...), custom_call_target="tpu_custom_call" | custom-call | flops 268435456 | bytes 1000000 | tf_op jit(solution)/shard_map/gate/pallas_call | solution.py:730
  112.6 2.2 %back.1 = (bf16[512,640]{1,0:T(8,128)(2,1)S(1)}, bf16[4,512,128]{2,1,0:T(8,128)(2,1)S(1)}, bf16[2,512,128]{2,1,0:T(8,128)(2,1)S(1)}, f32[2,512,128]{2,1,0:T(8,128)S(1)}) custom-call(s32[27]{0:T(128)S(1)} %concatenate.18.ints.ints_ref, f32[16,1024]{1,0:T(8,128)S(1)} %concatenate.21.vecs, bf16[2,544,128]{2,1,0:T(8,128)(2,1)S(1)} %get-tuple-element.186.refs_0_, ...), custom_call_target="tpu_custom_call" | custom-call | flops 134217728 | bytes 8000000 | tf_op jit(solution)/shard_map/back/pallas_call | solution.py:744
  114.8 1.1 back_own.1.mine
  115.9 1.0 collective-permute-done.37.theirs
  116.9 2.6 %out_2.2 = (bf16[128,2176]{1,0:T(8,128)(2,1)S(1)}, bf16[128,2176]{1,0:T(8,128)(2,1)S(1)}, bf16[1024,2048]{1,0:T(8,128)(2,1)S(1)}) custom-call(s32[27]{0:T(128)S(1)} %concatenate.18.ints.ints_ref, bf16[512,640]{1,0:T(8,128)(2,1)S(1)} %back_own.1.mine, bf16[512,640]{1,0:T(8,128)(2,1)S(1)} %collective-permute-done.37.theirs, ...), custom_call_target="tpu_custom_call" | custom-call | flops 1073741824 | bytes 8000000 | tf_op jit(solution)/shard_map/out_2/pallas_call | solution.py:782
  119.5 4.4 %collective-permute-start.38 = (bf16[128,2176]{1,0:T(8,128)(2,1)S(1)}, bf16[128,2176]{1,0:T(8,128)(2,1)S(1)}, u32[]{:S(2)}, u32[]{:S(2)}) collective-permute-start(bf16[128,2176]{1,0:T(8,128)(2,1)S(1)} %get-tuple-element.209.own), channel_id=1, source_target_pairs={{0,1},{3,2},{4,5},{7,6},{8,9},{11,10},{12,13},{15,14},{16,17},{19,... | collective-permute-start | bytes 1671176 | tf_op jit(solution)/shard_map/ppermute | solution.py:516
  123.9 1.9 %out_2.3 = (bf16[128,2176]{1,0:T(8,128)(2,1)S(1)}, f32[128,2176]{1,0:T(8,128)S(1)}) custom-call(s32[27]{0:T(128)S(1)} %concatenate.18.ints.ints_ref, bf16[512,640]{1,0:T(8,128)(2,1)S(1)} %back_own.1.mine, bf16[512,640]{1,0:T(8,128)(2,1)S(1)} %collective-permute-done.37.theirs, bf16[1024,2048]{1,0:T(8,128)(2,1)S(1)} %get-tuple-element.211.refs_0_), custom_call_target="tpu_custom_call" | custom-call | flops 1073741824 | bytes 8000000 | tf_op jit(solution)/shard_map/out_2/pallas_call | solution.py:782
  125.9 10.2 %collective-permute-done.38.got = bf16[128,2176]{1,0:T(8,128)(2,1)S(1)} collective-permute-done((bf16[128,2176]{1,0:T(8,128)(2,1)S(1)}, bf16[128,2176]{1,0:T(8,128)(2,1)S(1)}, u32[]{:S(2)}, u32[]{:S(2)}) %collective-permute-start.38) | collective-permute-done | bytes 557088 | tf_op jit(solution)/shard_map/ppermute | solution.py:516
  136.1 4.4 %collective-permute-start.40 = (bf16[128,2176]{1,0:T(8,128)(2,1)S(1)}, bf16[128,2176]{1,0:T(8,128)(2,1)S(1)}, u32[]{:S(2)}, u32[]{:S(2)}) collective-permute-start(bf16[128,2176]{1,0:T(8,128)(2,1)S(1)} %get-tuple-element.215.own), channel_id=1, source_target_pairs={{0,1},{3,2},{4,5},{7,6},{8,9},{11,10},{12,13},{15,14},{16,17},{19,... | collective-permute-start | bytes 1671176 | tf_op jit(solution)/shard_map/ppermute | solution.py:516
  140.5 1.3 collective-permute-start.39
  142.1 1.3 collective-permute-start.42
  143.4 8.4 %collective-permute-done.40.got = bf16[128,2176]{1,0:T(8,128)(2,1)S(1)} collective-permute-done((bf16[128,2176]{1,0:T(8,128)(2,1)S(1)}, bf16[128,2176]{1,0:T(8,128)(2,1)S(1)}, u32[]{:S(2)}, u32[]{:S(2)}) %collective-permute-start.40) | collective-permute-done | bytes 557088 | tf_op jit(solution)/shard_map/ppermute | solution.py:516
  152.1 0.7 collective-permute-start.43
  152.8 7.7 %collective-permute-start.41 = (bf16[128,2176]{1,0:T(8,128)(2,1)S(1)}, bf16[128,2176]{1,0:T(8,128)(2,1)S(1)}, u32[]{:S(2)}, u32[]{:S(2)}) collective-permute-start(bf16[128,2176]{1,0:T(8,128)(2,1)S(1)} %get-tuple-element.217), channel_id=1, source_target_pairs={{0,1},{3,2},{4,5},{7,6},{8,9},{11,10},{12,13},{15,14},{16,17},{19,... | collective-permute-start | bytes 1671176 | tf_op jit(solution)/shard_map/ppermute | solution.py:516
  160.6 1.5 collective-permute-done.44
  162.1 1.1 maximum_select_fusion
  163.2 4.7 %collective-permute-done.39.refs_0_ = bf16[128,2176]{1,0:T(8,128)(2,1)S(1)} collective-permute-done((bf16[128,2176]{1,0:T(8,128)(2,1)S(1)}, bf16[128,2176]{1,0:T(8,128)(2,1)S(1)}, u32[]{:S(2)}, u32[]{:S(2)}) %collective-permute-start.39) | collective-permute-done | bytes 557088 | tf_op jit(solution)/shard_map/ppermute | solution.py:516
  167.9 2.7 %collective-permute-done.41.refs_1_ = bf16[128,2176]{1,0:T(8,128)(2,1)S(1)} collective-permute-done((bf16[128,2176]{1,0:T(8,128)(2,1)S(1)}, bf16[128,2176]{1,0:T(8,128)(2,1)S(1)}, u32[]{:S(2)}, u32[]{:S(2)}) %collective-permute-start.41) | collective-permute-done | bytes 557088 | tf_op jit(solution)/shard_map/ppermute | solution.py:516
  170.6 1.2 final.1
  (85 shorter events, 9.4 us)
Async XLA Ops:
  0.6 15.0 %copy-start.7 = (f32[4,256]{1,0:T(4,128)S(1)}, f32[4,256]{1,0:T(4,128)}, u32[]{:S(2)}) copy-start(f32[4,256]{1,0:T(4,128)} %param.21) | copy-start | bytes 12292
  0.6 15.0 %copy-start.8 = (f32[256]{0:T(256)S(1)}, f32[256]{0:T(256)}, u32[]{:S(2)}) copy-start(f32[256]{0:T(256)} %param.22) | copy-start | bytes 3076
  0.7 15.0 %copy-start.5 = (f32[1024]{0:T(1024)S(1)}, f32[1024]{0:T(1024)}, u32[]{:S(2)}) copy-start(f32[1024]{0:T(1024)} %param.20) | copy-start | bytes 12292
  0.7 15.0 %copy-start.6 = (f32[1024]{0:T(1024)S(1)}, f32[1024]{0:T(1024)}, u32[]{:S(2)}) copy-start(f32[1024]{0:T(1024)} %param.26) | copy-start | bytes 12292
  0.7 15.0 %copy-start.4 = (f32[4,1024]{1,0:T(4,128)S(1)}, f32[4,1024]{1,0:T(4,128)}, u32[]{:S(2)}) copy-start(f32[4,1024]{1,0:T(4,128)} %param.19) | copy-start | bytes 49156
  0.7 15.0 %collective-permute-start.5 = (bf16[512,2048]{1,0:T(8,128)(2,1)}, bf16[512,2048]{1,0:T(8,128)(2,1)}, u32[]{:S(2)}, u32[]{:S(2)}) collective-permute-start(bf16[512,2048]{1,0:T(8,128)(2,1)} %param.15), channel_id=1, source_target_pairs={{0,4},{4,0},{8,12},{12,8},{16,20},{20,16},{24,28},{28,24},{1,5},{5... | collective-permute-start | bytes 6291464 | tf_op jit(solution)/shard_map/ppermute | solution.py:29
  2.5 20.8 %collective-permute-start.1 = (bf16[1024,256]{1,0:T(8,128)(2,1)S(1)}, bf16[1024,256]{1,0:T(8,128)(2,1)S(1)}, u32[]{:S(2)}, u32[]{:S(2)}) collective-permute-start(bf16[1024,256]{1,0:T(8,128)(2,1)S(1)} %convert_element_type.10.refs_0_), channel_id=1, source_target_pairs={{0,8},{4,12},{8,0},{12,4},{16,24},{20,28},{24,16},{28,20},{1,9},{5... | collective-permute-start | bytes 1572872 | tf_op jit(solution)/shard_map/ppermute | solution.py:29
  5.0 18.2 %collective-permute-start.2 = (bf16[1024,256]{1,0:T(8,128)(2,1)S(1)}, bf16[1024,256]{1,0:T(8,128)(2,1)S(1)}, u32[]{:S(2)}, u32[]{:S(2)}) collective-permute-start(bf16[1024,256]{1,0:T(8,128)(2,1)S(1)} %convert_element_type.10.refs_0_), channel_id=1, source_target_pairs={{0,16},{4,20},{8,24},{12,28},{16,0},{20,4},{24,8},{28,12},{1,17},{... | collective-permute-start | bytes 1572872 | tf_op jit(solution)/shard_map/ppermute | solution.py:29
  7.3 1.6 copy-start
  8.9 0.8 copy-start.2
  9.8 0.8 copy-start.3
  11.4 9.4 %collective-permute-start = (bf16[64,1408]{1,0:T(8,128)(2,1)S(1)}, bf16[64,1408]{1,0:T(8,128)(2,1)S(1)}, u32[]{:S(2)}, u32[]{:S(2)}) collective-permute-start(bf16[64,1408]{1,0:T(8,128)(2,1)S(1)} %get-tuple-element.113), channel_id=1, source_target_pairs={{0,1},{1,2},{2,3},{3,0},{4,5},{5,6},{6,7},{7,4},{8,9},{9,10},{10,1... | collective-permute-start | bytes 540680 | tf_op jit(solution)/shard_map/ppermute | solution.py:34
  13.0 14.5 %collective-permute-start.3 = (bf16[64,1408]{1,0:T(8,128)(2,1)S(1)}, bf16[64,1408]{1,0:T(8,128)(2,1)S(1)}, u32[]{:S(2)}, u32[]{:S(2)}) collective-permute-start(bf16[64,1408]{1,0:T(8,128)(2,1)S(1)} %get-tuple-element.115), channel_id=1, source_target_pairs={{0,2},{1,3},{2,0},{3,1},{4,6},{5,7},{6,4},{7,5},{8,10},{9,11},{10,... | collective-permute-start | bytes 540680 | tf_op jit(solution)/shard_map/ppermute | solution.py:34
  15.7 7.4 %copy-start.9 = (f32[16]{0:T(128)S(1)}, f32[16]{0:T(128)}, u32[]{:S(2)}) copy-start(f32[16]{0:T(128)} %param.25) | copy-start | bytes 196
  15.7 7.4 %copy-start.10 = (f32[16]{0:T(128)S(1)}, f32[16]{0:T(128)}, u32[]{:S(2)}) copy-start(f32[16]{0:T(128)} %param.24) | copy-start | bytes 196
  15.8 7.4 %copy-start.11 = (f32[16]{0:T(128)S(1)}, f32[16]{0:T(128)}, u32[]{:S(2)}) copy-start(f32[16]{0:T(128)} %param.23) | copy-start | bytes 196
  15.8 11.7 %collective-permute-start.4 = (bf16[64,1408]{1,0:T(8,128)(2,1)S(1)}, bf16[64,1408]{1,0:T(8,128)(2,1)S(1)}, u32[]{:S(2)}, u32[]{:S(2)}) collective-permute-start(bf16[64,1408]{1,0:T(8,128)(2,1)S(1)} %get-tuple-element.116), channel_id=1, source_target_pairs={{0,3},{1,0},{2,1},{3,2},{4,7},{5,4},{6,5},{7,6},{8,11},{9,8},{10,9... | collective-permute-start | bytes 540680 | tf_op jit(solution)/shard_map/ppermute | solution.py:34
  20.7 7.4 %collective-permute-start.6 = (bf16[16,2048]{1,0:T(8,128)(2,1)S(1)}, bf16[16,2048]{1,0:T(8,128)(2,1)S(1)}, u32[]{:S(2)}, u32[]{:S(2)}) collective-permute-start(bf16[16,2048]{1,0:T(8,128)(2,1)S(1)} %slice.28), channel_id=1, source_target_pairs={{0,8},{4,12},{8,16},{12,20},{16,24},{20,28},{1,9},{5,13},{9,17},{1... | collective-permute-start | bytes 196616 | tf_op jit(solution)/shard_map/ppermute | solution.py:633
  23.3 7.0 %collective-permute-start.7 = (bf16[512,256]{1,0:T(8,128)(2,1)S(1)}, bf16[512,256]{1,0:T(8,128)(2,1)S(1)}, u32[]{:S(2)}, u32[]{:S(2)}) collective-permute-start(bf16[512,256]{1,0:T(8,128)(2,1)S(1)} %slice.22), channel_id=1, source_target_pairs={{0,8},{4,12},{8,0},{12,4},{16,24},{20,28},{24,16},{28,20},{1,9},{5... | collective-permute-start | bytes 786440 | tf_op jit(solution)/shard_map/ppermute | solution.py:29
  24.8 6.5 %collective-permute-start.8 = (bf16[512,256]{1,0:T(8,128)(2,1)S(1)}, bf16[512,256]{1,0:T(8,128)(2,1)S(1)}, u32[]{:S(2)}, u32[]{:S(2)}) collective-permute-start(bf16[512,256]{1,0:T(8,128)(2,1)S(1)} %slice.23), channel_id=1, source_target_pairs={{0,16},{4,20},{8,24},{12,28},{16,0},{20,4},{24,8},{28,12},{1,17},{... | collective-permute-start | bytes 786440 | tf_op jit(solution)/shard_map/ppermute | solution.py:29
  28.1 4.0 %copy-start.1 = (f32[64,8192]{1,0:T(8,128)S(1)}, f32[64,8192]{1,0:T(8,128)}, u32[]{:S(2)}) copy-start(f32[64,8192]{1,0:T(8,128)} %w_ref.3) | copy-start | bytes 6291460
  31.3 25.8 %collective-permute-start.10 = (bf16[256,1408]{1,0:T(8,128)(2,1)S(1)}, bf16[256,1408]{1,0:T(8,128)(2,1)S(1)}, u32[]{:S(2)}, u32[]{:S(2)}) collective-permute-start(bf16[256,1408]{1,0:T(8,128)(2,1)S(1)} %assemble_x.1.refs_0_), channel_id=1, source_target_pairs={{0,16},{4,20},{8,24},{12,28},{16,0},{20,4},{24,8},{28,12},{1,17},{... | collective-permute-start | bytes 2162696 | tf_op jit(solution)/shard_map/ppermute | solution.py:29
  31.8 25.4 %collective-permute-start.9 = (bf16[256,1408]{1,0:T(8,128)(2,1)S(1)}, bf16[256,1408]{1,0:T(8,128)(2,1)S(1)}, u32[]{:S(2)}, u32[]{:S(2)}) collective-permute-start(bf16[256,1408]{1,0:T(8,128)(2,1)S(1)} %assemble_x.1.refs_0_), channel_id=1, source_target_pairs={{0,8},{4,12},{8,0},{12,4},{16,24},{20,28},{24,16},{28,20},{1,9},{5... | collective-permute-start | bytes 2162696 | tf_op jit(solution)/shard_map/ppermute | solution.py:29
  32.7 11.8 %collective-permute-start.11 = (bf16[64,1024]{1,0:T(8,128)(2,1)S(1)}, bf16[64,1024]{1,0:T(8,128)(2,1)S(1)}, u32[]{:S(2)}, u32[]{:S(2)}) collective-permute-start(bf16[64,1024]{1,0:T(8,128)(2,1)S(1)} %get-tuple-element.126), channel_id=1, source_target_pairs={{0,1},{1,2},{2,3},{3,0},{4,5},{5,6},{6,7},{7,4},{8,9},{9,10},{10,1... | collective-permute-start | bytes 393224 | tf_op jit(solution)/shard_map/ppermute | solution.py:34
  41.9 24.6 %collective-permute-start.16 = (bf16[256,1408]{1,0:T(8,128)(2,1)S(1)}, bf16[256,1408]{1,0:T(8,128)(2,1)S(1)}, u32[]{:S(2)}, u32[]{:S(2)}) collective-permute-start(bf16[256,1408]{1,0:T(8,128)(2,1)S(1)} %assemble_x.1.refs_0_), channel_id=1, source_target_pairs={{0,4},{4,0},{8,12},{12,8},{16,20},{20,16},{24,28},{28,24},{1,5},{5... | collective-permute-start | bytes 2162696 | tf_op jit(solution)/shard_map/ppermute | solution.py:29
  41.9 10.0 %collective-permute-start.12 = (bf16[64,1024]{1,0:T(8,128)(2,1)S(1)}, bf16[64,1024]{1,0:T(8,128)(2,1)S(1)}, u32[]{:S(2)}, u32[]{:S(2)}) collective-permute-start(bf16[64,1024]{1,0:T(8,128)(2,1)S(1)} %get-tuple-element.127), channel_id=1, source_target_pairs={{0,2},{1,3},{2,0},{3,1},{4,6},{5,7},{6,4},{7,5},{8,10},{9,11},{10,... | collective-permute-start | bytes 393224 | tf_op jit(solution)/shard_map/ppermute | solution.py:34
  44.5 12.7 %collective-permute-start.13 = (bf16[64,1024]{1,0:T(8,128)(2,1)S(1)}, bf16[64,1024]{1,0:T(8,128)(2,1)S(1)}, u32[]{:S(2)}, u32[]{:S(2)}) collective-permute-start(bf16[64,1024]{1,0:T(8,128)(2,1)S(1)} %get-tuple-element.128), channel_id=1, source_target_pairs={{0,3},{1,0},{2,1},{3,2},{4,7},{5,4},{6,5},{7,6},{8,11},{9,8},{10,9... | collective-permute-start | bytes 393224 | tf_op jit(solution)/shard_map/ppermute | solution.py:34
  57.2 7.5 %collective-permute-start.14 = (bf16[128,1408]{1,0:T(8,128)(2,1)S(1)}, bf16[128,1408]{1,0:T(8,128)(2,1)S(1)}, u32[]{:S(2)}, u32[]{:S(2)}) collective-permute-start(bf16[128,1408]{1,0:T(8,128)(2,1)S(1)} %slice.24), channel_id=1, source_target_pairs={{0,8},{4,12},{8,0},{12,4},{16,24},{20,28},{24,16},{28,20},{1,9},{5... | collective-permute-start | bytes 1081352 | tf_op jit(solution)/shard_map/ppermute | solution.py:29
  58.4 7.5 %collective-permute-start.15 = (bf16[128,1408]{1,0:T(8,128)(2,1)S(1)}, bf16[128,1408]{1,0:T(8,128)(2,1)S(1)}, u32[]{:S(2)}, u32[]{:S(2)}) collective-permute-start(bf16[128,1408]{1,0:T(8,128)(2,1)S(1)} %slice.25), channel_id=1, source_target_pairs={{0,16},{4,20},{8,24},{12,28},{16,0},{20,4},{24,8},{28,12},{1,17},{... | collective-permute-start | bytes 1081352 | tf_op jit(solution)/shard_map/ppermute | solution.py:29
  60.3 8.8 %collective-permute-start.17 = (bf16[256,1408]{1,0:T(8,128)(2,1)S(1)}, bf16[256,1408]{1,0:T(8,128)(2,1)S(1)}, u32[]{:S(2)}, u32[]{:S(2)}) collective-permute-start(bf16[256,1408]{1,0:T(8,128)(2,1)S(1)} %collective-permute-done.9.refs_1_), channel_id=1, source_target_pairs={{0,4},{4,0},{8,12},{12,8},{16,20},{20,16},{24,28},{28,24},{1,5},{5... | collective-permute-start | bytes 2162696 | tf_op jit(solution)/shard_map/ppermute | solution.py:29
  60.3 9.5 %collective-permute-start.18 = (bf16[256,1408]{1,0:T(8,128)(2,1)S(1)}, bf16[256,1408]{1,0:T(8,128)(2,1)S(1)}, u32[]{:S(2)}, u32[]{:S(2)}) collective-permute-start(bf16[256,1408]{1,0:T(8,128)(2,1)S(1)} %collective-permute-done.10.refs_2_), channel_id=1, source_target_pairs={{0,4},{4,0},{8,12},{12,8},{16,20},{20,16},{24,28},{28,24},{1,5},{5... | collective-permute-start | bytes 2162696 | tf_op jit(solution)/shard_map/ppermute | solution.py:29
  64.7 3.9 %collective-permute-start.19 = (bf16[128,1408]{1,0:T(8,128)(2,1)S(1)}, bf16[128,1408]{1,0:T(8,128)(2,1)S(1)}, u32[]{:S(2)}, u32[]{:S(2)}) collective-permute-start(bf16[128,1408]{1,0:T(8,128)(2,1)S(1)} %collective-permute-done.14.refs_3_), channel_id=1, source_target_pairs={{0,4},{4,0},{8,12},{12,8},{16,20},{20,16},{24,28},{28,24},{1,5},{5... | collective-permute-start | bytes 1081352 | tf_op jit(solution)/shard_map/ppermute | solution.py:29
  65.9 2.9 %collective-permute-start.20 = (bf16[128,1408]{1,0:T(8,128)(2,1)S(1)}, bf16[128,1408]{1,0:T(8,128)(2,1)S(1)}, u32[]{:S(2)}, u32[]{:S(2)}) collective-permute-start(bf16[128,1408]{1,0:T(8,128)(2,1)S(1)} %collective-permute-done.15.refs_4_), channel_id=1, source_target_pairs={{0,4},{4,0},{8,12},{12,8},{16,20},{20,16},{24,28},{28,24},{1,5},{5... | collective-permute-start | bytes 1081352 | tf_op jit(solution)/shard_map/ppermute | solution.py:29
  66.5 1.7 %collective-permute-start.21 = (bf16[256,512]{1,0:T(8,128)(2,1)S(1)}, bf16[256,512]{1,0:T(8,128)(2,1)S(1)}, u32[]{:S(2)}, u32[]{:S(2)}) collective-permute-start(bf16[256,512]{1,0:T(8,128)(2,1)S(1)} %get-tuple-element.136), channel_id=1, source_target_pairs={{0,4},{4,0},{8,12},{12,8},{16,20},{20,16},{24,28},{28,24},{1,5},{5... | collective-permute-start | bytes 786440 | tf_op jit(solution)/shard_map/ppermute | solution.py:29
  68.2 12.0 %collective-permute-start.26 = (bf16[1024,256]{1,0:T(8,128)(2,1)S(1)}, bf16[1024,256]{1,0:T(8,128)(2,1)S(1)}, u32[]{:S(2)}, u32[]{:S(2)}) collective-permute-start(bf16[1024,256]{1,0:T(8,128)(2,1)S(1)} %convert_element_type.10.refs_0_), channel_id=1, source_target_pairs={{0,4},{4,0},{8,12},{12,8},{16,20},{20,16},{24,28},{28,24},{1,5},{5... | collective-permute-start | bytes 1572872 | tf_op jit(solution)/shard_map/ppermute | solution.py:29
  68.6 13.1 %collective-permute-start.27 = (bf16[1024,256]{1,0:T(8,128)(2,1)S(1)}, bf16[1024,256]{1,0:T(8,128)(2,1)S(1)}, u32[]{:S(2)}, u32[]{:S(2)}) collective-permute-start(bf16[1024,256]{1,0:T(8,128)(2,1)S(1)} %collective-permute-done.1.refs_1_), channel_id=1, source_target_pairs={{0,4},{4,0},{8,12},{12,8},{16,20},{20,16},{24,28},{28,24},{1,5},{5... | collective-permute-start | bytes 1572872 | tf_op jit(solution)/shard_map/ppermute | solution.py:29
  68.8 2.5 %collective-permute-start.29 = (bf16[512,256]{1,0:T(8,128)(2,1)S(1)}, bf16[512,256]{1,0:T(8,128)(2,1)S(1)}, u32[]{:S(2)}, u32[]{:S(2)}) collective-permute-start(bf16[512,256]{1,0:T(8,128)(2,1)S(1)} %collective-permute-done.7.refs_3_), channel_id=1, source_target_pairs={{0,4},{4,0},{8,12},{12,8},{16,20},{20,16},{24,28},{28,24},{1,5},{5... | collective-permute-start | bytes 786440 | tf_op jit(solution)/shard_map/ppermute | solution.py:29
  69.1 3.1 %collective-permute-start.30 = (bf16[512,256]{1,0:T(8,128)(2,1)S(1)}, bf16[512,256]{1,0:T(8,128)(2,1)S(1)}, u32[]{:S(2)}, u32[]{:S(2)}) collective-permute-start(bf16[512,256]{1,0:T(8,128)(2,1)S(1)} %collective-permute-done.8.refs_4_), channel_id=1, source_target_pairs={{0,4},{4,0},{8,12},{12,8},{16,20},{20,16},{24,28},{28,24},{1,5},{5... | collective-permute-start | bytes 786440 | tf_op jit(solution)/shard_map/ppermute | solution.py:29
  69.9 17.7 %collective-permute-start.28 = (bf16[1024,256]{1,0:T(8,128)(2,1)S(1)}, bf16[1024,256]{1,0:T(8,128)(2,1)S(1)}, u32[]{:S(2)}, u32[]{:S(2)}) collective-permute-start(bf16[1024,256]{1,0:T(8,128)(2,1)S(1)} %collective-permute-done.2.refs_2_), channel_id=1, source_target_pairs={{0,4},{4,0},{8,12},{12,8},{16,20},{20,16},{24,28},{28,24},{1,5},{5... | collective-permute-start | bytes 1572872 | tf_op jit(solution)/shard_map/ppermute | solution.py:29
  71.3 20.8 %collective-permute-start.24 = (bf16[512,512]{1,0:T(8,128)(2,1)S(1)}, bf16[512,512]{1,0:T(8,128)(2,1)S(1)}, u32[]{:S(2)}, u32[]{:S(2)}) collective-permute-start(bf16[512,512]{1,0:T(8,128)(2,1)S(1)} %merge_z.1.refs_0_), channel_id=1, source_target_pairs={{0,8},{4,12},{8,0},{12,4},{16,24},{20,28},{24,16},{28,20},{1,9},{5... | collective-permute-start | bytes 1572872 | tf_op jit(solution)/shard_map/ppermute | solution.py:29
  72.2 19.9 %collective-permute-start.25 = (bf16[512,512]{1,0:T(8,128)(2,1)S(1)}, bf16[512,512]{1,0:T(8,128)(2,1)S(1)}, u32[]{:S(2)}, u32[]{:S(2)}) collective-permute-start(bf16[512,512]{1,0:T(8,128)(2,1)S(1)} %merge_z.1.refs_0_), channel_id=1, source_target_pairs={{0,16},{4,20},{8,24},{12,28},{16,0},{20,4},{24,8},{28,12},{1,17},{... | collective-permute-start | bytes 1572872 | tf_op jit(solution)/shard_map/ppermute | solution.py:29
  80.2 11.2 %collective-permute-start.22 = (bf16[2,544,128]{2,1,0:T(8,128)(2,1)S(1)}, bf16[2,544,128]{2,1,0:T(8,128)(2,1)S(1)}, u32[]{:S(2)}, u32[]{:S(2)}) collective-permute-start(bf16[2,544,128]{2,1,0:T(8,128)(2,1)S(1)} %get-tuple-element.186.refs_0_), channel_id=1, source_target_pairs={{0,8},{4,12},{8,0},{12,4},{16,24},{20,28},{24,16},{28,20},{1,9},{5... | collective-permute-start | bytes 835592 | tf_op jit(solution)/shard_map/ppermute | solution.py:29
  81.7 10.4 %collective-permute-start.23 = (bf16[2,544,128]{2,1,0:T(8,128)(2,1)S(1)}, bf16[2,544,128]{2,1,0:T(8,128)(2,1)S(1)}, u32[]{:S(2)}, u32[]{:S(2)}) collective-permute-start(bf16[2,544,128]{2,1,0:T(8,128)(2,1)S(1)} %get-tuple-element.186.refs_0_), channel_id=1, source_target_pairs={{0,16},{4,20},{8,24},{12,28},{16,0},{20,4},{24,8},{28,12},{1,17},{... | collective-permute-start | bytes 835592 | tf_op jit(solution)/shard_map/ppermute | solution.py:29
  92.1 9.6 %collective-permute-start.31 = (bf16[2,544,128]{2,1,0:T(8,128)(2,1)S(1)}, bf16[2,544,128]{2,1,0:T(8,128)(2,1)S(1)}, u32[]{:S(2)}, u32[]{:S(2)}) collective-permute-start(bf16[2,544,128]{2,1,0:T(8,128)(2,1)S(1)} %get-tuple-element.187.refs_1_), channel_id=1, source_target_pairs={{0,8},{4,12},{8,0},{12,4},{16,24},{20,28},{24,16},{28,20},{1,9},{5... | collective-permute-start | bytes 835592 | tf_op jit(solution)/shard_map/ppermute | solution.py:29
  93.3 9.6 %collective-permute-start.32 = (bf16[2,544,128]{2,1,0:T(8,128)(2,1)S(1)}, bf16[2,544,128]{2,1,0:T(8,128)(2,1)S(1)}, u32[]{:S(2)}, u32[]{:S(2)}) collective-permute-start(bf16[2,544,128]{2,1,0:T(8,128)(2,1)S(1)} %get-tuple-element.187.refs_1_), channel_id=1, source_target_pairs={{0,16},{4,20},{8,24},{12,28},{16,0},{20,4},{24,8},{28,12},{1,17},{... | collective-permute-start | bytes 835592 | tf_op jit(solution)/shard_map/ppermute | solution.py:29
  95.1 12.2 %collective-permute-start.35 = (bf16[256,512]{1,0:T(8,128)(2,1)S(1)}, bf16[256,512]{1,0:T(8,128)(2,1)S(1)}, u32[]{:S(2)}, u32[]{:S(2)}) collective-permute-start(bf16[256,512]{1,0:T(8,128)(2,1)S(1)} %slice.26), channel_id=1, source_target_pairs={{0,8},{4,12},{8,0},{12,4},{16,24},{20,28},{24,16},{28,20},{1,9},{5... | collective-permute-start | bytes 786440 | tf_op jit(solution)/shard_map/ppermute | solution.py:29
  95.8 12.7 %collective-permute-start.36 = (bf16[256,512]{1,0:T(8,128)(2,1)S(1)}, bf16[256,512]{1,0:T(8,128)(2,1)S(1)}, u32[]{:S(2)}, u32[]{:S(2)}) collective-permute-start(bf16[256,512]{1,0:T(8,128)(2,1)S(1)} %slice.27), channel_id=1, source_target_pairs={{0,16},{4,20},{8,24},{12,28},{16,0},{20,4},{24,8},{28,12},{1,17},{... | collective-permute-start | bytes 786440 | tf_op jit(solution)/shard_map/ppermute | solution.py:29
  98.8 13.8 %collective-permute-start.33 = (bf16[2,544,128]{2,1,0:T(8,128)(2,1)S(1)}, bf16[2,544,128]{2,1,0:T(8,128)(2,1)S(1)}, u32[]{:S(2)}, u32[]{:S(2)}) collective-permute-start(bf16[2,544,128]{2,1,0:T(8,128)(2,1)S(1)} %collective-permute-done.23.refs_4_), channel_id=1, source_target_pairs={{0,8},{4,12},{8,0},{12,4},{16,24},{20,28},{24,16},{28,20},{1,9},{5... | collective-permute-start | bytes 835592 | tf_op jit(solution)/shard_map/ppermute | solution.py:29
  102.9 9.6 %collective-permute-start.34 = (bf16[2,544,128]{2,1,0:T(8,128)(2,1)S(1)}, bf16[2,544,128]{2,1,0:T(8,128)(2,1)S(1)}, u32[]{:S(2)}, u32[]{:S(2)}) collective-permute-start(bf16[2,544,128]{2,1,0:T(8,128)(2,1)S(1)} %collective-permute-done.31.refs_3_), channel_id=1, source_target_pairs={{0,16},{4,20},{8,24},{12,28},{16,0},{20,4},{24,8},{28,12},{1,17},{... | collective-permute-start | bytes 835592 | tf_op jit(solution)/shard_map/ppermute | solution.py:29
  114.7 2.2 %collective-permute-start.37 = (bf16[512,640]{1,0:T(8,128)(2,1)S(1)}, bf16[512,640]{1,0:T(8,128)(2,1)S(1)}, u32[]{:S(2)}, u32[]{:S(2)}) collective-permute-start(bf16[512,640]{1,0:T(8,128)(2,1)S(1)} %get-tuple-element.203), channel_id=1, source_target_pairs={{0,4},{4,0},{8,12},{12,8},{16,20},{20,16},{24,28},{28,24},{1,5},{5... | collective-permute-start | bytes 1966088 | tf_op jit(solution)/shard_map/ppermute | solution.py:29
  119.5 16.6 %collective-permute-start.38 = (bf16[128,2176]{1,0:T(8,128)(2,1)S(1)}, bf16[128,2176]{1,0:T(8,128)(2,1)S(1)}, u32[]{:S(2)}, u32[]{:S(2)}) collective-permute-start(bf16[128,2176]{1,0:T(8,128)(2,1)S(1)} %get-tuple-element.209.own), channel_id=1, source_target_pairs={{0,1},{3,2},{4,5},{7,6},{8,9},{11,10},{12,13},{15,14},{16,17},{19,... | collective-permute-start | bytes 1671176 | tf_op jit(solution)/shard_map/ppermute | solution.py:516
  136.1 15.7 %collective-permute-start.40 = (bf16[128,2176]{1,0:T(8,128)(2,1)S(1)}, bf16[128,2176]{1,0:T(8,128)(2,1)S(1)}, u32[]{:S(2)}, u32[]{:S(2)}) collective-permute-start(bf16[128,2176]{1,0:T(8,128)(2,1)S(1)} %get-tuple-element.215.own), channel_id=1, source_target_pairs={{0,1},{3,2},{4,5},{7,6},{8,9},{11,10},{12,13},{15,14},{16,17},{19,... | collective-permute-start | bytes 1671176 | tf_op jit(solution)/shard_map/ppermute | solution.py:516
  140.5 27.4 %collective-permute-start.39 = (bf16[128,2176]{1,0:T(8,128)(2,1)S(1)}, bf16[128,2176]{1,0:T(8,128)(2,1)S(1)}, u32[]{:S(2)}, u32[]{:S(2)}) collective-permute-start(bf16[128,2176]{1,0:T(8,128)(2,1)S(1)} %get-tuple-element.217), channel_id=1, source_target_pairs={{1,0},{2,3},{5,4},{6,7},{9,8},{10,11},{13,12},{14,15},{17,16},{18,... | collective-permute-start | bytes 1671176 | tf_op jit(solution)/shard_map/ppermute | solution.py:516
  142.1 25.8 %collective-permute-start.42 = (bf16[128,2176]{1,0:T(8,128)(2,1)S(1)}, bf16[128,2176]{1,0:T(8,128)(2,1)S(1)}, u32[]{:S(2)}, u32[]{:S(2)}) collective-permute-start(bf16[128,2176]{1,0:T(8,128)(2,1)S(1)} %add_far.1), channel_id=1, source_target_pairs={{1,3},{2,0},{5,7},{6,4},{9,11},{10,8},{13,15},{14,12},{17,19},{18,... | collective-permute-start | bytes 1671176 | tf_op jit(solution)/shard_map/ppermute | solution.py:516
  152.1 15.8 %collective-permute-start.43 = (bf16[128,2176]{1,0:T(8,128)(2,1)S(1)}, bf16[128,2176]{1,0:T(8,128)(2,1)S(1)}, u32[]{:S(2)}, u32[]{:S(2)}) collective-permute-start(bf16[128,2176]{1,0:T(8,128)(2,1)S(1)} %add_mid.1), channel_id=1, source_target_pairs={{1,2},{2,1},{5,6},{6,5},{9,10},{10,9},{13,14},{14,13},{17,18},{18,... | collective-permute-start | bytes 1671176 | tf_op jit(solution)/shard_map/ppermute | solution.py:516
  152.8 17.8 %collective-permute-start.41 = (bf16[128,2176]{1,0:T(8,128)(2,1)S(1)}, bf16[128,2176]{1,0:T(8,128)(2,1)S(1)}, u32[]{:S(2)}, u32[]{:S(2)}) collective-permute-start(bf16[128,2176]{1,0:T(8,128)(2,1)S(1)} %get-tuple-element.217), channel_id=1, source_target_pairs={{0,1},{3,2},{4,5},{7,6},{8,9},{11,10},{12,13},{15,14},{16,17},{19,... | collective-permute-start | bytes 1671176 | tf_op jit(solution)/shard_map/ppermute | solution.py:516
  160.5 1.6 collective-permute-start.44
where the time goes:
time: 172 us
  starting transfers between devices  68.2 us (40%)
  waiting for transfers between devices  59.1 us (34%)
  Pallas kernels  33.9 us (20%)
  other arithmetic  5.39 us (3%)
  local copies, waits for them, and re-layouts  4.19 us (2%)
    ppermute x6, waiting for transfers between devices, send(): return lax.ppermute(x, 'tp', pairs)  26 us
    ppermute x32, starting transfers between devices, flip(): return lax.ppermute(x, 'seq', [(i, i ^ bits) for i in range(count)])  24.1 us
    ppermute x6, starting transfers between devices, shift(): return lax.ppermute(x, 'tp', [(i, (i + by) % count) for i in range(count)])  21.9 us
    ppermute x32, waiting for transfers between devices, flip(): return lax.ppermute(x, 'seq', [(i, i ^ bits) for i in range(count)])  21.3 us
    ppermute x6, starting transfers between devices, send(): return lax.ppermute(x, 'tp', pairs)  19.8 us
    pallas_call x2, Pallas kernels, front(): call(functools.partial(front_kernel, (inner, bc_width, heads, prompts, wh...  12.1 us
    ppermute x6, waiting for transfers between devices, shift(): return lax.ppermute(x, 'tp', [(i, (i + by) % count) for i in range(count)])  11.8 us
    pallas_call x2, Pallas kernels, mid(): call(functools.partial(mid_kernel, (inner, heads, prompts, groups, side))...  4.89 us
  transfers between devices with their start and end apart: 45, of which 22 were waited for; matrix products, arithmetic and copies ran while one was open for 4% of the time, Pallas kernels for 16%

commit v1 on v0

--- a/solution.py
+++ b/solution.py
@@ -441,8 +441,19 @@
 
 def block_places(t, tp_count):
     if tp_count == 4:
-        return [jnp.where(t < 2, 3, 0), jnp.where(t < 2, 2, 1), t ^ 1, t]
+        inside = is_inner(t)
+        far, mid, near = jnp.where(t < 2, 3, 0), jnp.where(t < 2, 2, 1), t ^ 1
+        return [
+            jnp.where(inside, near, far),
+            jnp.where(inside, far, mid),
+            jnp.where(inside, mid, near),
+            t,
+        ]
     return [lax.rem(t + j, tp_count) for j in range(1, tp_count)] + [t]
+
+
+def is_inner(t):
+    return (t == 1) | (t == 2)
 
 
 def out_kernel(sizes, ints, mine, theirs, *refs):
@@ -484,50 +495,61 @@
             out[:, lanes] = value.astype(out.dtype)
 
 
-def add_kernel(got, own, out):
+def add_kernel(ints, got, own, out):
     width = out.shape[1] - LANES
+    inside = is_inner(ints[0])
     for at in range(0, width, 512):
         lanes = slice(at, at + 512)
-        out[:, lanes] = (got[:, lanes].astype(F32) + own[:, lanes].astype(F32)).astype(MM)
-    out[:, width:] = spread_terms(added_terms(got, width) + added_terms(own, width)).astype(MM)
-
-
-def final_kernel(channels, own, *refs):
+        came = jnp.where(inside, got[:, lanes].astype(F32), 0.0)
+        out[:, lanes] = (came + own[:, lanes].astype(F32)).astype(MM)
+    came = jnp.where(inside, added_terms(got, width), 0.0)
+    out[:, width:] = spread_terms(came + added_terms(own, width)).astype(MM)
+
+
+def final_kernel(channels, at_ends, ints, own, *refs):
     received, out = refs[:-1], refs[-1]
     width = out.shape[1]
+    inside = is_inner(ints[0])
+
+    def taken(value, where):
+        if where is None:
+            return value
+        return jnp.where(inside, 0.0, value) if where else jnp.where(inside, value, 0.0)
+
     squares = added_terms(own, width)
-    for got in received:
-        squares = squares + added_terms(got, width)
+    for got, where in zip(received, at_ends):
+        squares = squares + taken(added_terms(got, width), where)
     factor = lax.rsqrt(squares[:, :1] / channels + epsilon)
     for at in range(0, width, 512):
         lanes = slice(at, at + 512)
         total = own[:, lanes]
-        for got in received:
-            total = total + got[:, lanes].astype(F32)
+        for got, where in zip(received, at_ends):
+            total = total + taken(got[:, lanes].astype(F32), where)
         out[:, lanes] = (total * factor).astype(out.dtype)
 
 
-def sum_over_tp(blocks, own):
+def sum_over_tp(ints, blocks, own):
     tp_count = lax.axis_size("tp")
     if tp_count != 4:
-        return own, [shift(x, j + 1) for j, x in enumerate(blocks)]
+        return own, [shift(x, j + 1) for j, x in enumerate(blocks)], (None,) * (tp_count - 1)
 
     def send(x, pairs):
         return lax.ppermute(x, "tp", pairs)
 
     def add(got, x, name):
-        return call(add_kernel, [sds(x.shape, MM)], [VMEM] * 2, moved=1_700_000, name=name)(got, x)[0]
-
-    far, mid, near = blocks
-    far_got = send(far, [(0, 1), (3, 2)])
-    to_end = send(near, [(1, 0), (2, 3)])
-    far_got, mid, near, own = lax.optimization_barrier((far_got, mid, near, own))
-    mid_got = send(mid, [(0, 1), (3, 2)])
-    far_sum = send(add(far_got, far, "add_far"), [(1, 3), (2, 0)])
-    mid_got, near = lax.optimization_barrier((mid_got, near))
-    to_inner = send(near, [(0, 1), (3, 2)])
-    mid_sum = send(add(mid_got, mid, "add_mid"), [(1, 2), (2, 1)])
-    return own, [to_end, to_inner, far_sum, mid_sum]
+        specs = [SMEM, VMEM, VMEM]
+        return call(add_kernel, [sds(x.shape, MM)], specs, moved=1_700_000, name=name)(ints, got, x)[0]
+
+    first, second, third = blocks
+    from_near = send(first, [(0, 1), (1, 0), (2, 3), (3, 2)])
+    from_near, third, own = lax.optimization_barrier((from_near, third, own))
+    second = add(from_near, second, "add_far")
+    second, third = lax.optimization_barrier((second, third))
+    from_second = send(second, [(0, 1), (3, 2), (1, 3), (2, 0)])
+    from_end = send(third, [(0, 1), (3, 2)])
+    third = add(from_second, third, "add_mid")
+    from_middle = send(third, [(1, 2), (2, 1), (0, 0), (3, 3)])
+    return own, [from_near, from_second, from_end, from_middle], (True, True, False, False)
 
 
 def on_device(
@@ -619,25 +641,26 @@
 
     out_near = plane_near(w_out.astype(MM))
     keys = list(out_near)
-    x_got[1:2], out_got = together(x_got[1:2], [out_near[k][0] for k in keys])
+    other = flip(tokens, 1)
+    first_tok = jnp.where(c == 0, tokens, other)
+    second_tok = jnp.where(c == 0, other, tokens)
+    out_got, (first_tok, second_tok) = together(
+        [out_near[k][0] for k in keys], [first_tok, second_tok]
+    )
     out_blocks = plane_far({k: (piece,) for k, piece in zip(keys, out_got)})
     out_own = [piece for k in out_blocks for piece in out_blocks[k]]
     out_where = [
         (k, 0, i * (w_out.shape[0] // 2)) for k in out_blocks for i in range(len(out_blocks[k]))
     ]
+    x_got, out_own = together(x_got, out_own)
     (x_block,) = assembled(assemble_x_kernel, [sds((depth, x_width), MM)], x_got, "assemble_x")
 
-    other = flip(tokens, 1)
-    first_tok = jnp.where(c == 0, tokens, other)
-    second_tok = jnp.where(c == 0, other, tokens)
     before = lax.ppermute(
         second_tok[tok_dev - HALO :], "seq", [(i, i + 2) for i in range(seq_count - 2)]
     )
     all_tok = jnp.concatenate([before, first_tok, second_tok], axis=0)
 
-    (x_block, all_tok, ints, floats, vecs), out_own = together(
-        [x_block, all_tok, ints, floats, vecs], out_own
-    )
+    ((x_block, all_tok, ints, floats, vecs),) = together([x_block, all_tok, ints, floats, vecs])
     near = plane_near(x_block)
     z_sent = packed(
         pack_z_kernel,
@@ -795,13 +818,13 @@
     near_block, own = project_out(
         (ahead, ahead + 1), [block, sds(block.shape, F32)], (), [out_weights]
     )
-    own, received = sum_over_tp([*sent_first, near_block], own)
+    own, received, at_ends = sum_over_tp(ints, [*sent_first, near_block], own)
     (mixed,) = call(
-        functools.partial(final_kernel, float(inner_all)),
+        functools.partial(final_kernel, float(inner_all), at_ends),
         [sds((piece, out_width), MM)],
-        [VMEM] * (1 + len(received)),
+        [SMEM] + [VMEM] * (1 + len(received)),
         name="final",
-    )(own, *received)
+    )(ints, own, *received)
 
     other_asked = flip(asked, 1).astype(F32)
     states = jnp.where(

time: 172 us -> 163 us (0.948)
  the two profiles are of different devices: /device:TPU:0 before, /device:TPU:16 now
where the time goes in v1:
time: 163 us; the launch traced here: 162 us
  waiting for transfers between devices  78.5 us (48%)
  starting transfers between devices  37.7 us (23%)
  Pallas kernels  35.4 us (22%)
  other arithmetic  5.37 us (3%)
  local copies, waits for them, and re-layouts  4.19 us (3%)
    ppermute x4, waiting for transfers between devices, send(): return lax.ppermute(x, 'tp', pairs)  35.5 us
    ppermute x32, waiting for transfers between devices, flip(): return lax.ppermute(x, 'seq', [(i, i ^ bits) for i in range(count)])  29.9 us
    ppermute x32, starting transfers between devices, flip(): return lax.ppermute(x, 'seq', [(i, i ^ bits) for i in range(count)])  26.6 us
    ppermute x6, waiting for transfers between devices, shift(): return lax.ppermute(x, 'tp', [(i, (i + by) % count) for i in range(count)])  13.1 us
    pallas_call x2, Pallas kernels, front(): call(functools.partial(front_kernel, (inner, bc_width, heads, prompts, wh...  12.2 us
    ppermute x6, starting transfers between devices, shift(): return lax.ppermute(x, 'tp', [(i, (i + by) % count) for i in range(count)])  5.33 us
    pallas_call x2, Pallas kernels, mid(): call(functools.partial(mid_kernel, (inner, heads, prompts, groups, side))...  4.9 us
    pallas_call x2, Pallas kernels, project_out(): call(functools.partial(out_kernel, (inner, tp_count, chosen, where)), out...  4.35 us
  transfers between devices with their start and end apart: 43, of which 23 were waited for; matrix products, arithmetic and copies ran while one was open for 4% of the time, Pallas kernels for 17%

profile of v1, /device:TPU:16, one launch (start us, length us, event | category | flops | bytes accessed | tf_op | source)
XLA Modules:
  0.0 162.3 jit_solution(11685811242221063150)
XLA Ops:
  0.8 1.3 convert_element_type.10.refs_0_
  2.0 1.6 collective-permute-start.3
  3.6 1.5 collective-permute-start.4
  5.1 0.7 concatenate.18.ints.ints_ref
  5.9 1.6 copy-done
  7.5 0.8 copy-done.2
  8.3 0.8 copy-done.3
  9.1 0.9 pack_x.1
  9.9 1.6 %collective-permute-start = (bf16[64,1408]{1,0:T(8,128)(2,1)S(1)}, bf16[64,1408]{1,0:T(8,128)(2,1)S(1)}, u32[]{:S(2)}, u32[]{:S(2)}) collective-permute-start(bf16[64,1408]{1,0:T(8,128)(2,1)S(1)} %get-tuple-element.117), channel_id=1, source_target_pairs={{0,1},{1,2},{2,3},{3,0},{4,5},{5,6},{6,7},{7,4},{8,9},{9,10},{10,1... | collective-permute-start | bytes 540680 | tf_op jit(solution)/shard_map/ppermute | solution.py:34
  12.1 1.4 collective-permute-start.2
  13.5 2.5 %broadcast_select_fusion = (bf16[512,2048]{1,0:T(8,128)(2,1)S(1)}, bf16[512,2048]{1,0:T(8,128)(2,1)S(1)}) fusion(bf16[512,2048]{1,0:T(8,128)(2,1)} %collective-permute-done.5, bf16[512,2048]{1,0:T(8,128)(2,1)} %param.15, pred[]{:T(512)S(6)} %eq.4), kind=kLoop, calls=%fused_computation.1 | loop fusion | flops 2097152 | bytes 8388609 | tf_op jit(solution)/shard_map/jit(_where)/select_n | solution.py:646
  16.4 1.2 collective-permute-done.4.refs_2_
  17.6 2.4 %collective-permute-start.8 = (bf16[16,2048]{1,0:T(8,128)(2,1)S(1)}, bf16[16,2048]{1,0:T(8,128)(2,1)S(1)}, u32[]{:S(2)}, u32[]{:S(2)}) collective-permute-start(bf16[16,2048]{1,0:T(8,128)(2,1)S(1)} %slice.23), channel_id=1, source_target_pairs={{0,8},{4,12},{8,16},{12,20},{16,24},{20,28},{1,9},{5,13},{9,17},{1... | collective-permute-start | bytes 196616 | tf_op jit(solution)/shard_map/ppermute | solution.py:658
  20.2 2.5 %collective-permute-start.6 = (bf16[512,256]{1,0:T(8,128)(2,1)S(1)}, bf16[512,256]{1,0:T(8,128)(2,1)S(1)}, u32[]{:S(2)}, u32[]{:S(2)}) collective-permute-start(bf16[512,256]{1,0:T(8,128)(2,1)S(1)} %slice.21), channel_id=1, source_target_pairs={{0,8},{4,12},{8,0},{12,4},{16,24},{20,28},{24,16},{28,20},{1,9},{5... | collective-permute-start | bytes 786440 | tf_op jit(solution)/shard_map/ppermute | solution.py:29
  22.8 4.2 %collective-permute-start.7 = (bf16[512,256]{1,0:T(8,128)(2,1)S(1)}, bf16[512,256]{1,0:T(8,128)(2,1)S(1)}, u32[]{:S(2)}, u32[]{:S(2)}) collective-permute-start(bf16[512,256]{1,0:T(8,128)(2,1)S(1)} %slice.22), channel_id=1, source_target_pairs={{0,16},{4,20},{8,24},{12,28},{16,0},{20,4},{24,8},{28,12},{1,17},{... | collective-permute-start | bytes 786440 | tf_op jit(solution)/shard_map/ppermute | solution.py:29
  27.4 2.1 %collective-permute-done.6.refs_3_ = bf16[512,256]{1,0:T(8,128)(2,1)S(1)} collective-permute-done((bf16[512,256]{1,0:T(8,128)(2,1)S(1)}, bf16[512,256]{1,0:T(8,128)(2,1)S(1)}, u32[]{:S(2)}, u32[]{:S(2)}) %collective-permute-start.6) | collective-permute-done | bytes 262176 | tf_op jit(solution)/shard_map/ppermute | solution.py:29
  29.5 1.8 %collective-permute-done.7.refs_4_ = bf16[512,256]{1,0:T(8,128)(2,1)S(1)} collective-permute-done((bf16[512,256]{1,0:T(8,128)(2,1)S(1)}, bf16[512,256]{1,0:T(8,128)(2,1)S(1)}, u32[]{:S(2)}, u32[]{:S(2)}) %collective-permute-start.7) | collective-permute-done | bytes 262176 | tf_op jit(solution)/shard_map/ppermute | solution.py:29
  31.3 0.6 assemble_x.1.refs_0_
  31.9 2.4 %collective-permute-start.10 = (bf16[256,1408]{1,0:T(8,128)(2,1)S(1)}, bf16[256,1408]{1,0:T(8,128)(2,1)S(1)}, u32[]{:S(2)}, u32[]{:S(2)}) collective-permute-start(bf16[256,1408]{1,0:T(8,128)(2,1)S(1)} %assemble_x.1.refs_0_), channel_id=1, source_target_pairs={{0,16},{4,20},{8,24},{12,28},{16,0},{20,4},{24,8},{28,12},{1,17},{... | collective-permute-start | bytes 2162696 | tf_op jit(solution)/shard_map/ppermute | solution.py:29
  34.4 0.6 pack_z.1
  35.0 1.6 collective-permute-start.11
  36.9 8.1 %collective-permute-done.11.refs_1_ = bf16[64,1024]{1,0:T(8,128)(2,1)S(1)} collective-permute-done((bf16[64,1024]{1,0:T(8,128)(2,1)S(1)}, bf16[64,1024]{1,0:T(8,128)(2,1)S(1)}, u32[]{:S(2)}, u32[]{:S(2)}) %collective-permute-start.11) | collective-permute-done | bytes 131104 | tf_op jit(solution)/shard_map/ppermute | solution.py:34
  45.1 5.0 %collective-permute-done.13.refs_3_ = bf16[64,1024]{1,0:T(8,128)(2,1)S(1)} collective-permute-done((bf16[64,1024]{1,0:T(8,128)(2,1)S(1)}, bf16[64,1024]{1,0:T(8,128)(2,1)S(1)}, u32[]{:S(2)}, u32[]{:S(2)}) %collective-permute-start.13) | collective-permute-done | bytes 131104 | tf_op jit(solution)/shard_map/ppermute | solution.py:34
  50.1 0.5 collective-permute-start.18
  50.6 2.1 %collective-permute-start.14 = (bf16[128,1408]{1,0:T(8,128)(2,1)S(1)}, bf16[128,1408]{1,0:T(8,128)(2,1)S(1)}, u32[]{:S(2)}, u32[]{:S(2)}) collective-permute-start(bf16[128,1408]{1,0:T(8,128)(2,1)S(1)} %slice.24), channel_id=1, source_target_pairs={{0,8},{4,12},{8,0},{12,4},{16,24},{20,28},{24,16},{28,20},{1,9},{5... | collective-permute-start | bytes 1081352 | tf_op jit(solution)/shard_map/ppermute | solution.py:29
  52.9 8.5 %collective-permute-done.14.refs_3_ = bf16[128,1408]{1,0:T(8,128)(2,1)S(1)} collective-permute-done((bf16[128,1408]{1,0:T(8,128)(2,1)S(1)}, bf16[128,1408]{1,0:T(8,128)(2,1)S(1)}, u32[]{:S(2)}, u32[]{:S(2)}) %collective-permute-start.14) | collective-permute-done | bytes 360480 | tf_op jit(solution)/shard_map/ppermute | solution.py:29
  61.4 0.6 assemble_z.1
  62.0 0.6 collective-permute-start.21
  62.9 0.8 collective-permute-done.21.theirs
  64.7 0.6 merge_z.1.refs_0_
  65.8 1.0 collective-permute-done.29.refs_8_
  66.7 1.8 %collective-permute-start.24 = (bf16[512,512]{1,0:T(8,128)(2,1)S(1)}, bf16[512,512]{1,0:T(8,128)(2,1)S(1)}, u32[]{:S(2)}, u32[]{:S(2)}) collective-permute-start(bf16[512,512]{1,0:T(8,128)(2,1)S(1)} %merge_z.1.refs_0_), channel_id=1, source_target_pairs={{0,8},{4,12},{8,0},{12,4},{16,24},{20,28},{24,16},{28,20},{1,9},{5... | collective-permute-start | bytes 1572872 | tf_op jit(solution)/shard_map/ppermute | solution.py:29
  68.6 6.5 %front_0.1 = (bf16[512,512]{1,0:T(8,128)(2,1)S(1)}, bf16[512,256]{1,0:T(8,128)(2,1)S(1)}, f32[512,128]{1,0:T(8,128)S(1)}, f32[512,128]{1,0:T(8,128)S(1)}, bf16[2...) custom-call(s32[27]{0:T(128)S(1)} %concatenate.18.ints.ints_ref, f32[48]{0:T(128)S(1)} %pad_maximum_fusion.1.floats, ...), custom_call_target="tpu_custom_call" | custom-call | flops 1937768448 | bytes 8000000 | tf_op jit(solution)/shard_map/front_0/pallas_call | solution.py:700
  75.5 1.9 %collective-permute-start.23 = (bf16[2,544,128]{2,1,0:T(8,128)(2,1)S(1)}, bf16[2,544,128]{2,1,0:T(8,128)(2,1)S(1)}, u32[]{:S(2)}, u32[]{:S(2)}) collective-permute-start(bf16[2,544,128]{2,1,0:T(8,128)(2,1)S(1)} %get-tuple-element.195.refs_0_), channel_id=1, source_target_pairs={{0,16},{4,20},{8,24},{12,28},{16,0},{20,4},{24,8},{28,12},{1,17},{... | collective-permute-start | bytes 835592 | tf_op jit(solution)/shard_map/ppermute | solution.py:29
  77.4 5.7 %front_1.1 = (bf16[512,512]{1,0:T(8,128)(2,1)S(1)}, bf16[512,256]{1,0:T(8,128)(2,1)S(1)}, f32[512,128]{1,0:T(8,128)S(1)}, f32[512,128]{1,0:T(8,128)S(1)}, bf16[2,544,128]{2,1,0:T(8,128)(2,1)S(1)}) custom-call(s32[27]{0:T(128)S(1)} %concatenate.18.ints.ints_ref, f32[48]{0:T(128)S(1)} %pad_maximum_fusion.1.floats, f32[16,1024]{1,0:T(8,128)S(1)} %concatenate.21.vecs, ...), custom_call_target="tpu_custom_call" | custom-call | flops 1937768448 | bytes 8000000 | tf_op jit(solution)/shard_map/front_1/pallas_call | solution.py:700
  83.1 3.8 %collective-permute-done.22.refs_2_ = bf16[2,544,128]{2,1,0:T(8,128)(2,1)S(1)} collective-permute-done((bf16[2,544,128]{2,1,0:T(8,128)(2,1)S(1)}, bf16[2,544,128]{2,1,0:T(8,128)(2,1)S(1)}, u32[]{:S(2)}, u32[]{:S(2)}) %collective-permute-start.22) | collective-permute-done | bytes 278560 | tf_op jit(solution)/shard_map/ppermute | solution.py:29
  86.9 1.5 collective-permute-done.23.refs_4_
  88.4 0.7 collective-permute-start.31
  89.3 1.4 collective-permute-start.35
  90.8 1.8 %collective-permute-start.36 = (bf16[256,512]{1,0:T(8,128)(2,1)S(1)}, bf16[256,512]{1,0:T(8,128)(2,1)S(1)}, u32[]{:S(2)}, u32[]{:S(2)}) collective-permute-start(bf16[256,512]{1,0:T(8,128)(2,1)S(1)} %slice.27), channel_id=1, source_target_pairs={{0,16},{4,20},{8,24},{12,28},{16,0},{20,4},{24,8},{28,12},{1,17},{... | collective-permute-start | bytes 786440 | tf_op jit(solution)/shard_map/ppermute | solution.py:29
  92.6 2.4 %mid_0.1 = (f32[512,512]{1,0:T(8,128)S(1)}, f32[512,512]{1,0:T(8,128)S(1)}) custom-call(s32[27]{0:T(128)S(1)} %concatenate.18.ints.ints_ref, f32[48]{0:T(128)S(1)} %pad_maximum_fusion.1.floats, bf16[512,512]{1,0:T(8,128)(2,1)S(1)} %get-tuple-element.171.xs_ref, bf16[512,256]{1,0:T(8,128)(2,1)S(1)} %get-tuple-element.206.bc_ref.refs_11_.refs_3_, ...), custom_call_target="tpu_custom_call" | custom-call | flops 134217728 | bytes 1000000 | tf_op jit(solution)/shard_map/mid_0/pallas_call | solution.py:732
  95.0 0.7 collective-permute-start.33
  95.8 2.2 %collective-permute-done.31.refs_3_ = bf16[2,544,128]{2,1,0:T(8,128)(2,1)S(1)} collective-permute-done((bf16[2,544,128]{2,1,0:T(8,128)(2,1)S(1)}, bf16[2,544,128]{2,1,0:T(8,128)(2,1)S(1)}, u32[]{:S(2)}, u32[]{:S(2)}) %collective-permute-start.31) | collective-permute-done | bytes 278560 | tf_op jit(solution)/shard_map/ppermute | solution.py:29
  98.0 0.7 collective-permute-done.32.refs_5_
  98.9 2.5 %mid_1.1 = (f32[512,512]{1,0:T(8,128)S(1)}, f32[512,512]{1,0:T(8,128)S(1)}) custom-call(s32[27]{0:T(128)S(1)} %concatenate.18.ints.ints_ref, f32[48]{0:T(128)S(1)} %pad_maximum_fusion.1.floats, bf16[512,512]{1,0:T(8,128)(2,1)S(1)} %get-tuple-element.188.xs_ref, bf16[512,256]{1,0:T(8,128)(2,1)S(1)} %get-tuple-element.210.bc_ref.refs_15_.refs_7_, ...), custom_call_target="tpu_custom_call" | custom-call | flops 134217728 | bytes 1000000 | tf_op jit(solution)/shard_map/mid_1/pallas_call | solution.py:732
  101.4 2.2 %collective-permute-done.35.refs_3_ = bf16[256,512]{1,0:T(8,128)(2,1)S(1)} collective-permute-done((bf16[256,512]{1,0:T(8,128)(2,1)S(1)}, bf16[256,512]{1,0:T(8,128)(2,1)S(1)}, u32[]{:S(2)}, u32[]{:S(2)}) %collective-permute-start.35) | collective-permute-done | bytes 262176 | tf_op jit(solution)/shard_map/ppermute | solution.py:29
  103.6 0.7 collective-permute-done.36.refs_4_
  104.2 3.9 %gate.1 = (f32[512,512]{1,0:T(8,128)S(1)}, f32[512,512]{1,0:T(8,128)S(1)}) custom-call(s32[27]{0:T(128)S(1)} %concatenate.18.ints.ints_ref, bf16[1040,2048]{1,0:T(8,128)(2,1)S(1)} %pad_maximum_fusion.tok_ref, bf16[512,512]{1,0:T(8,128)(2,1)S(1)} %merge_z.1.refs_0_, bf16[512,512]{1,0:T(8,128)(2,1)S(1)} %collective-permute-done.24.refs_1_, ...), custom_call_target="tpu_custom_call" | custom-call | flops 268435456 | bytes 1000000 | tf_op jit(solution)/shard_map/gate/pallas_call | solution.py:753
  108.4 2.2 %back.1 = (bf16[512,640]{1,0:T(8,128)(2,1)S(1)}, bf16[4,512,128]{2,1,0:T(8,128)(2,1)S(1)}, bf16[2,512,128]{2,1,0:T(8,128)(2,1)S(1)}, f32[2,512,128]{2,1,0:T(8,128)S(1)}) custom-call(s32[27]{0:T(128)S(1)} %concatenate.18.ints.ints_ref, f32[16,1024]{1,0:T(8,128)S(1)} %concatenate.21.vecs, bf16[2,544,128]{2,1,0:T(8,128)(2,1)S(1)} %get-tuple-element.195.refs_0_, ...), custom_call_target="tpu_custom_call" | custom-call | flops 134217728 | bytes 8000000 | tf_op jit(solution)/shard_map/back/pallas_call | solution.py:767
  110.7 1.1 back_own.1.mine
  111.9 1.0 collective-permute-done.37.theirs
  112.8 2.5 %out_2.2 = (bf16[128,2176]{1,0:T(8,128)(2,1)S(1)}, bf16[128,2176]{1,0:T(8,128)(2,1)S(1)}, bf16[1024,2048]{1,0:T(8,128)(2,1)S(1)}) custom-call(s32[27]{0:T(128)S(1)} %concatenate.18.ints.ints_ref, bf16[512,640]{1,0:T(8,128)(2,1)S(1)} %back_own.1.mine, bf16[512,640]{1,0:T(8,128)(2,1)S(1)} %collective-permute-done.37.theirs, ...), custom_call_target="tpu_custom_call" | custom-call | flops 1073741824 | bytes 8000000 | tf_op jit(solution)/shard_map/out_2/pallas_call | solution.py:805
  115.4 1.8 %out_2.3 = (bf16[128,2176]{1,0:T(8,128)(2,1)S(1)}, f32[128,2176]{1,0:T(8,128)S(1)}) custom-call(s32[27]{0:T(128)S(1)} %concatenate.18.ints.ints_ref, bf16[512,640]{1,0:T(8,128)(2,1)S(1)} %back_own.1.mine, bf16[512,640]{1,0:T(8,128)(2,1)S(1)} %collective-permute-done.37.theirs, bf16[1024,2048]{1,0:T(8,128)(2,1)S(1)} %get-tuple-element.219.refs_0_), custom_call_target="tpu_custom_call" | custom-call | flops 1073741824 | bytes 8000000 | tf_op jit(solution)/shard_map/out_2/pallas_call | solution.py:805
  117.2 12.8 %collective-permute-done.38.got.refs_0_ = bf16[128,2176]{1,0:T(8,128)(2,1)S(1)} collective-permute-done((bf16[128,2176]{1,0:T(8,128)(2,1)S(1)}, bf16[128,2176]{1,0:T(8,128)(2,1)S(1)}, u32[]{:S(2)}, u32[]{:S(2)}) %collective-permute-start.38) | collective-permute-done | bytes 557088 | tf_op jit(solution)/shard_map/ppermute | solution.py:537
  130.1 0.8 add_far.1
  131.0 1.3 collective-permute-start.40
  132.3 14.2 %collective-permute-done.39.got.refs_1_ = bf16[128,2176]{1,0:T(8,128)(2,1)S(1)} collective-permute-done((bf16[128,2176]{1,0:T(8,128)(2,1)S(1)}, bf16[128,2176]{1,0:T(8,128)(2,1)S(1)}, u32[]{:S(2)}, u32[]{:S(2)}) %collective-permute-start.39) | collective-permute-done | bytes 557088 | tf_op jit(solution)/shard_map/ppermute | solution.py:537
  146.5 0.8 add_mid.1
  147.3 1.9 %collective-permute-start.41 = (bf16[128,2176]{1,0:T(8,128)(2,1)S(1)}, bf16[128,2176]{1,0:T(8,128)(2,1)S(1)}, u32[]{:S(2)}, u32[]{:S(2)}) collective-permute-start(bf16[128,2176]{1,0:T(8,128)(2,1)S(1)} %add_mid.1), channel_id=1, source_target_pairs={{1,2},{2,1},{0,0},{3,3},{5,6},{6,5},{4,4},{7,7},{9,10},{10,9},{8,8... | collective-permute-start | bytes 1671176 | tf_op jit(solution)/shard_map/ppermute | solution.py:537
  149.3 1.5 collective-permute-done.42
  150.9 1.1 maximum_select_fusion
  152.0 4.7 %collective-permute-done.40.refs_2_ = bf16[128,2176]{1,0:T(8,128)(2,1)S(1)} collective-permute-done((bf16[128,2176]{1,0:T(8,128)(2,1)S(1)}, bf16[128,2176]{1,0:T(8,128)(2,1)S(1)}, u32[]{:S(2)}, u32[]{:S(2)}) %collective-permute-start.40) | collective-permute-done | bytes 557088 | tf_op jit(solution)/shard_map/ppermute | solution.py:537
  156.7 3.7 %collective-permute-done.41.refs_3_ = bf16[128,2176]{1,0:T(8,128)(2,1)S(1)} collective-permute-done((bf16[128,2176]{1,0:T(8,128)(2,1)S(1)}, bf16[128,2176]{1,0:T(8,128)(2,1)S(1)}, u32[]{:S(2)}, u32[]{:S(2)}) %collective-permute-start.41) | collective-permute-done | bytes 557088 | tf_op jit(solution)/shard_map/ppermute | solution.py:537
  160.4 1.9 %final.1 = bf16[128,2048]{1,0:T(8,128)(2,1)} custom-call(s32[27]{0:T(128)S(1)} %concatenate.18.ints.ints_ref, f32[128,2176]{1,0:T(8,128)S(1)} %get-tuple-element.222.own, bf16[128,2176]{1,0:T(8,128)(2,1)S(1)} %collective-permute-done.38.got.refs_0_, bf16[128,2176]{1,0:T(8,128)(2,1)S(1)} %collective-permute-done.39.got.refs_1_, ...), custom_call_target="tpu_custom_call" | custom-call | tf_op jit(solution)/shard_map/final/pallas_call | solution.py:822
  (81 shorter events, 5.7 us)
Async XLA Ops:
  0.6 11.3 %copy-start.7 = (f32[4,256]{1,0:T(4,128)S(1)}, f32[4,256]{1,0:T(4,128)}, u32[]{:S(2)}) copy-start(f32[4,256]{1,0:T(4,128)} %param.21) | copy-start | bytes 12292
  0.6 11.3 %copy-start.8 = (f32[256]{0:T(256)S(1)}, f32[256]{0:T(256)}, u32[]{:S(2)}) copy-start(f32[256]{0:T(256)} %param.22) | copy-start | bytes 3076
  0.7 11.3 %copy-start.5 = (f32[1024]{0:T(1024)S(1)}, f32[1024]{0:T(1024)}, u32[]{:S(2)}) copy-start(f32[1024]{0:T(1024)} %param.20) | copy-start | bytes 12292
  0.7 11.3 %copy-start.6 = (f32[1024]{0:T(1024)S(1)}, f32[1024]{0:T(1024)}, u32[]{:S(2)}) copy-start(f32[1024]{0:T(1024)} %param.26) | copy-start | bytes 12292
  0.7 11.3 %copy-start.4 = (f32[4,1024]{1,0:T(4,128)S(1)}, f32[4,1024]{1,0:T(4,128)}, u32[]{:S(2)}) copy-start(f32[4,1024]{1,0:T(4,128)} %param.19) | copy-start | bytes 49156
  0.7 11.3 %collective-permute-start.5 = (bf16[512,2048]{1,0:T(8,128)(2,1)}, bf16[512,2048]{1,0:T(8,128)(2,1)}, u32[]{:S(2)}, u32[]{:S(2)}) collective-permute-start(bf16[512,2048]{1,0:T(8,128)(2,1)} %param.15), channel_id=1, source_target_pairs={{0,4},{4,0},{8,12},{12,8},{16,20},{20,16},{24,28},{28,24},{1,5},{5... | collective-permute-start | bytes 6291464 | tf_op jit(solution)/shard_map/ppermute | solution.py:29
  2.0 14.4 %collective-permute-start.3 = (bf16[1024,256]{1,0:T(8,128)(2,1)S(1)}, bf16[1024,256]{1,0:T(8,128)(2,1)S(1)}, u32[]{:S(2)}, u32[]{:S(2)}) collective-permute-start(bf16[1024,256]{1,0:T(8,128)(2,1)S(1)} %convert_element_type.10.refs_0_), channel_id=1, source_target_pairs={{0,8},{4,12},{8,0},{12,4},{16,24},{20,28},{24,16},{28,20},{1,9},{5... | collective-permute-start | bytes 1572872 | tf_op jit(solution)/shard_map/ppermute | solution.py:29
  3.6 14.0 %collective-permute-start.4 = (bf16[1024,256]{1,0:T(8,128)(2,1)S(1)}, bf16[1024,256]{1,0:T(8,128)(2,1)S(1)}, u32[]{:S(2)}, u32[]{:S(2)}) collective-permute-start(bf16[1024,256]{1,0:T(8,128)(2,1)S(1)} %convert_element_type.10.refs_0_), channel_id=1, source_target_pairs={{0,16},{4,20},{8,24},{12,28},{16,0},{20,4},{24,8},{28,12},{1,17},{... | collective-permute-start | bytes 1572872 | tf_op jit(solution)/shard_map/ppermute | solution.py:29
  5.9 1.6 copy-start
  7.5 0.8 copy-start.2
  8.3 0.8 copy-start.3
  9.9 17.4 %collective-permute-start = (bf16[64,1408]{1,0:T(8,128)(2,1)S(1)}, bf16[64,1408]{1,0:T(8,128)(2,1)S(1)}, u32[]{:S(2)}, u32[]{:S(2)}) collective-permute-start(bf16[64,1408]{1,0:T(8,128)(2,1)S(1)} %get-tuple-element.117), channel_id=1, source_target_pairs={{0,1},{1,2},{2,3},{3,0},{4,5},{5,6},{6,7},{7,4},{8,9},{9,10},{10,1... | collective-permute-start | bytes 540680 | tf_op jit(solution)/shard_map/ppermute | solution.py:34
  11.5 15.8 %collective-permute-start.1 = (bf16[64,1408]{1,0:T(8,128)(2,1)S(1)}, bf16[64,1408]{1,0:T(8,128)(2,1)S(1)}, u32[]{:S(2)}, u32[]{:S(2)}) collective-permute-start(bf16[64,1408]{1,0:T(8,128)(2,1)S(1)} %get-tuple-element.118), channel_id=1, source_target_pairs={{0,2},{1,3},{2,0},{3,1},{4,6},{5,7},{6,4},{7,5},{8,10},{9,11},{10,... | collective-permute-start | bytes 540680 | tf_op jit(solution)/shard_map/ppermute | solution.py:34
  12.0 8.1 %copy-start.9 = (f32[16]{0:T(128)S(1)}, f32[16]{0:T(128)}, u32[]{:S(2)}) copy-start(f32[16]{0:T(128)} %param.25) | copy-start | bytes 196
  12.0 8.1 %copy-start.10 = (f32[16]{0:T(128)S(1)}, f32[16]{0:T(128)}, u32[]{:S(2)}) copy-start(f32[16]{0:T(128)} %param.24) | copy-start | bytes 196
  12.1 8.1 %copy-start.11 = (f32[16]{0:T(128)S(1)}, f32[16]{0:T(128)}, u32[]{:S(2)}) copy-start(f32[16]{0:T(128)} %param.23) | copy-start | bytes 196
  12.1 15.3 %collective-permute-start.2 = (bf16[64,1408]{1,0:T(8,128)(2,1)S(1)}, bf16[64,1408]{1,0:T(8,128)(2,1)S(1)}, u32[]{:S(2)}, u32[]{:S(2)}) collective-permute-start(bf16[64,1408]{1,0:T(8,128)(2,1)S(1)} %get-tuple-element.119), channel_id=1, source_target_pairs={{0,3},{1,0},{2,1},{3,2},{4,7},{5,4},{6,5},{7,6},{8,11},{9,8},{10,9... | collective-permute-start | bytes 540680 | tf_op jit(solution)/shard_map/ppermute | solution.py:34
  17.6 5.1 %collective-permute-start.8 = (bf16[16,2048]{1,0:T(8,128)(2,1)S(1)}, bf16[16,2048]{1,0:T(8,128)(2,1)S(1)}, u32[]{:S(2)}, u32[]{:S(2)}) collective-permute-start(bf16[16,2048]{1,0:T(8,128)(2,1)S(1)} %slice.23), channel_id=1, source_target_pairs={{0,8},{4,12},{8,16},{12,20},{16,24},{20,28},{1,9},{5,13},{9,17},{1... | collective-permute-start | bytes 196616 | tf_op jit(solution)/shard_map/ppermute | solution.py:658
  20.2 9.3 %collective-permute-start.6 = (bf16[512,256]{1,0:T(8,128)(2,1)S(1)}, bf16[512,256]{1,0:T(8,128)(2,1)S(1)}, u32[]{:S(2)}, u32[]{:S(2)}) collective-permute-start(bf16[512,256]{1,0:T(8,128)(2,1)S(1)} %slice.21), channel_id=1, source_target_pairs={{0,8},{4,12},{8,0},{12,4},{16,24},{20,28},{24,16},{28,20},{1,9},{5... | collective-permute-start | bytes 786440 | tf_op jit(solution)/shard_map/ppermute | solution.py:29
  22.8 11.6 %copy-start.1 = (f32[64,8192]{1,0:T(8,128)S(1)}, f32[64,8192]{1,0:T(8,128)}, u32[]{:S(2)}) copy-start(f32[64,8192]{1,0:T(8,128)} %w_ref.3) | copy-start | bytes 6291460
  22.8 8.6 %collective-permute-start.7 = (bf16[512,256]{1,0:T(8,128)(2,1)S(1)}, bf16[512,256]{1,0:T(8,128)(2,1)S(1)}, u32[]{:S(2)}, u32[]{:S(2)}) collective-permute-start(bf16[512,256]{1,0:T(8,128)(2,1)S(1)} %slice.22), channel_id=1, source_target_pairs={{0,16},{4,20},{8,24},{12,28},{16,0},{20,4},{24,8},{28,12},{1,17},{... | collective-permute-start | bytes 786440 | tf_op jit(solution)/shard_map/ppermute | solution.py:29
  31.9 18.1 %collective-permute-start.10 = (bf16[256,1408]{1,0:T(8,128)(2,1)S(1)}, bf16[256,1408]{1,0:T(8,128)(2,1)S(1)}, u32[]{:S(2)}, u32[]{:S(2)}) collective-permute-start(bf16[256,1408]{1,0:T(8,128)(2,1)S(1)} %assemble_x.1.refs_0_), channel_id=1, source_target_pairs={{0,16},{4,20},{8,24},{12,28},{16,0},{20,4},{24,8},{28,12},{1,17},{... | collective-permute-start | bytes 2162696 | tf_op jit(solution)/shard_map/ppermute | solution.py:29
  34.4 15.7 %collective-permute-start.9 = (bf16[256,1408]{1,0:T(8,128)(2,1)S(1)}, bf16[256,1408]{1,0:T(8,128)(2,1)S(1)}, u32[]{:S(2)}, u32[]{:S(2)}) collective-permute-start(bf16[256,1408]{1,0:T(8,128)(2,1)S(1)} %assemble_x.1.refs_0_), channel_id=1, source_target_pairs={{0,8},{4,12},{8,0},{12,4},{16,24},{20,28},{24,16},{28,20},{1,9},{5... | collective-permute-start | bytes 2162696 | tf_op jit(solution)/shard_map/ppermute | solution.py:29
  35.0 10.1 %collective-permute-start.11 = (bf16[64,1024]{1,0:T(8,128)(2,1)S(1)}, bf16[64,1024]{1,0:T(8,128)(2,1)S(1)}, u32[]{:S(2)}, u32[]{:S(2)}) collective-permute-start(bf16[64,1024]{1,0:T(8,128)(2,1)S(1)} %get-tuple-element.135), channel_id=1, source_target_pairs={{0,1},{1,2},{2,3},{3,0},{4,5},{5,6},{6,7},{7,4},{8,9},{9,10},{10,1... | collective-permute-start | bytes 393224 | tf_op jit(solution)/shard_map/ppermute | solution.py:34
  36.5 25.4 %collective-permute-start.16 = (bf16[256,1408]{1,0:T(8,128)(2,1)S(1)}, bf16[256,1408]{1,0:T(8,128)(2,1)S(1)}, u32[]{:S(2)}, u32[]{:S(2)}) collective-permute-start(bf16[256,1408]{1,0:T(8,128)(2,1)S(1)} %assemble_x.1.refs_0_), channel_id=1, source_target_pairs={{0,4},{4,0},{8,12},{12,8},{16,20},{20,16},{24,28},{28,24},{1,5},{5... | collective-permute-start | bytes 2162696 | tf_op jit(solution)/shard_map/ppermute | solution.py:29
  36.5 8.6 %collective-permute-start.12 = (bf16[64,1024]{1,0:T(8,128)(2,1)S(1)}, bf16[64,1024]{1,0:T(8,128)(2,1)S(1)}, u32[]{:S(2)}, u32[]{:S(2)}) collective-permute-start(bf16[64,1024]{1,0:T(8,128)(2,1)S(1)} %get-tuple-element.136), channel_id=1, source_target_pairs={{0,2},{1,3},{2,0},{3,1},{4,6},{5,7},{6,4},{7,5},{8,10},{9,11},{10,... | collective-permute-start | bytes 393224 | tf_op jit(solution)/shard_map/ppermute | solution.py:34
  45.1 5.0 %collective-permute-start.13 = (bf16[64,1024]{1,0:T(8,128)(2,1)S(1)}, bf16[64,1024]{1,0:T(8,128)(2,1)S(1)}, u32[]{:S(2)}, u32[]{:S(2)}) collective-permute-start(bf16[64,1024]{1,0:T(8,128)(2,1)S(1)} %get-tuple-element.137), channel_id=1, source_target_pairs={{0,3},{1,0},{2,1},{3,2},{4,7},{5,4},{6,5},{7,6},{8,11},{9,8},{10,9... | collective-permute-start | bytes 393224 | tf_op jit(solution)/shard_map/ppermute | solution.py:34
  50.1 14.0 %collective-permute-start.17 = (bf16[256,1408]{1,0:T(8,128)(2,1)S(1)}, bf16[256,1408]{1,0:T(8,128)(2,1)S(1)}, u32[]{:S(2)}, u32[]{:S(2)}) collective-permute-start(bf16[256,1408]{1,0:T(8,128)(2,1)S(1)} %collective-permute-done.9.refs_1_), channel_id=1, source_target_pairs={{0,4},{4,0},{8,12},{12,8},{16,20},{20,16},{24,28},{28,24},{1,5},{5... | collective-permute-start | bytes 2162696 | tf_op jit(solution)/shard_map/ppermute | solution.py:29
  50.1 14.1 %collective-permute-start.18 = (bf16[256,1408]{1,0:T(8,128)(2,1)S(1)}, bf16[256,1408]{1,0:T(8,128)(2,1)S(1)}, u32[]{:S(2)}, u32[]{:S(2)}) collective-permute-start(bf16[256,1408]{1,0:T(8,128)(2,1)S(1)} %collective-permute-done.10.refs_2_), channel_id=1, source_target_pairs={{0,4},{4,0},{8,12},{12,8},{16,20},{20,16},{24,28},{28,24},{1,5},{5... | collective-permute-start | bytes 2162696 | tf_op jit(solution)/shard_map/ppermute | solution.py:29
  50.6 10.7 %collective-permute-start.14 = (bf16[128,1408]{1,0:T(8,128)(2,1)S(1)}, bf16[128,1408]{1,0:T(8,128)(2,1)S(1)}, u32[]{:S(2)}, u32[]{:S(2)}) collective-permute-start(bf16[128,1408]{1,0:T(8,128)(2,1)S(1)} %slice.24), channel_id=1, source_target_pairs={{0,8},{4,12},{8,0},{12,4},{16,24},{20,28},{24,16},{28,20},{1,9},{5... | collective-permute-start | bytes 1081352 | tf_op jit(solution)/shard_map/ppermute | solution.py:29
  52.7 10.2 %collective-permute-start.15 = (bf16[128,1408]{1,0:T(8,128)(2,1)S(1)}, bf16[128,1408]{1,0:T(8,128)(2,1)S(1)}, u32[]{:S(2)}, u32[]{:S(2)}) collective-permute-start(bf16[128,1408]{1,0:T(8,128)(2,1)S(1)} %slice.25), channel_id=1, source_target_pairs={{0,16},{4,20},{8,24},{12,28},{16,0},{20,4},{24,8},{28,12},{1,17},{... | collective-permute-start | bytes 1081352 | tf_op jit(solution)/shard_map/ppermute | solution.py:29
  61.3 3.2 %collective-permute-start.19 = (bf16[128,1408]{1,0:T(8,128)(2,1)S(1)}, bf16[128,1408]{1,0:T(8,128)(2,1)S(1)}, u32[]{:S(2)}, u32[]{:S(2)}) collective-permute-start(bf16[128,1408]{1,0:T(8,128)(2,1)S(1)} %collective-permute-done.14.refs_3_), channel_id=1, source_target_pairs={{0,4},{4,0},{8,12},{12,8},{16,20},{20,16},{24,28},{28,24},{1,5},{5... | collective-permute-start | bytes 1081352 | tf_op jit(solution)/shard_map/ppermute | solution.py:29
  62.0 1.7 %collective-permute-start.21 = (bf16[256,512]{1,0:T(8,128)(2,1)S(1)}, bf16[256,512]{1,0:T(8,128)(2,1)S(1)}, u32[]{:S(2)}, u32[]{:S(2)}) collective-permute-start(bf16[256,512]{1,0:T(8,128)(2,1)S(1)} %get-tuple-element.145), channel_id=1, source_target_pairs={{0,4},{4,0},{8,12},{12,8},{16,20},{20,16},{24,28},{28,24},{1,5},{5... | collective-permute-start | bytes 786440 | tf_op jit(solution)/shard_map/ppermute | solution.py:29
  62.9 2.4 %collective-permute-start.20 = (bf16[128,1408]{1,0:T(8,128)(2,1)S(1)}, bf16[128,1408]{1,0:T(8,128)(2,1)S(1)}, u32[]{:S(2)}, u32[]{:S(2)}) collective-permute-start(bf16[128,1408]{1,0:T(8,128)(2,1)S(1)} %collective-permute-done.15.refs_4_), channel_id=1, source_target_pairs={{0,4},{4,0},{8,12},{12,8},{16,20},{20,16},{24,28},{28,24},{1,5},{5... | collective-permute-start | bytes 1081352 | tf_op jit(solution)/shard_map/ppermute | solution.py:29
  63.7 11.4 %collective-permute-start.26 = (bf16[1024,256]{1,0:T(8,128)(2,1)S(1)}, bf16[1024,256]{1,0:T(8,128)(2,1)S(1)}, u32[]{:S(2)}, u32[]{:S(2)}) collective-permute-start(bf16[1024,256]{1,0:T(8,128)(2,1)S(1)} %convert_element_type.10.refs_0_), channel_id=1, source_target_pairs={{0,4},{4,0},{8,12},{12,8},{16,20},{20,16},{24,28},{28,24},{1,5},{5... | collective-permute-start | bytes 1572872 | tf_op jit(solution)/shard_map/ppermute | solution.py:29
  64.1 11.4 %collective-permute-start.27 = (bf16[1024,256]{1,0:T(8,128)(2,1)S(1)}, bf16[1024,256]{1,0:T(8,128)(2,1)S(1)}, u32[]{:S(2)}, u32[]{:S(2)}) collective-permute-start(bf16[1024,256]{1,0:T(8,128)(2,1)S(1)} %collective-permute-done.3.refs_1_), channel_id=1, source_target_pairs={{0,4},{4,0},{8,12},{12,8},{16,20},{20,16},{24,28},{28,24},{1,5},{5... | collective-permute-start | bytes 1572872 | tf_op jit(solution)/shard_map/ppermute | solution.py:29
  64.2 2.5 %collective-permute-start.29 = (bf16[512,256]{1,0:T(8,128)(2,1)S(1)}, bf16[512,256]{1,0:T(8,128)(2,1)S(1)}, u32[]{:S(2)}, u32[]{:S(2)}) collective-permute-start(bf16[512,256]{1,0:T(8,128)(2,1)S(1)} %collective-permute-done.6.refs_3_), channel_id=1, source_target_pairs={{0,4},{4,0},{8,12},{12,8},{16,20},{20,16},{24,28},{28,24},{1,5},{5... | collective-permute-start | bytes 786440 | tf_op jit(solution)/shard_map/ppermute | solution.py:29
  64.6 3.9 %collective-permute-start.30 = (bf16[512,256]{1,0:T(8,128)(2,1)S(1)}, bf16[512,256]{1,0:T(8,128)(2,1)S(1)}, u32[]{:S(2)}, u32[]{:S(2)}) collective-permute-start(bf16[512,256]{1,0:T(8,128)(2,1)S(1)} %collective-permute-done.7.refs_4_), channel_id=1, source_target_pairs={{0,4},{4,0},{8,12},{12,8},{16,20},{20,16},{24,28},{28,24},{1,5},{5... | collective-permute-start | bytes 786440 | tf_op jit(solution)/shard_map/ppermute | solution.py:29
  65.3 17.8 %collective-permute-start.28 = (bf16[1024,256]{1,0:T(8,128)(2,1)S(1)}, bf16[1024,256]{1,0:T(8,128)(2,1)S(1)}, u32[]{:S(2)}, u32[]{:S(2)}) collective-permute-start(bf16[1024,256]{1,0:T(8,128)(2,1)S(1)} %collective-permute-done.4.refs_2_), channel_id=1, source_target_pairs={{0,4},{4,0},{8,12},{12,8},{16,20},{20,16},{24,28},{28,24},{1,5},{5... | collective-permute-start | bytes 1572872 | tf_op jit(solution)/shard_map/ppermute | solution.py:29
  66.7 21.6 %collective-permute-start.24 = (bf16[512,512]{1,0:T(8,128)(2,1)S(1)}, bf16[512,512]{1,0:T(8,128)(2,1)S(1)}, u32[]{:S(2)}, u32[]{:S(2)}) collective-permute-start(bf16[512,512]{1,0:T(8,128)(2,1)S(1)} %merge_z.1.refs_0_), channel_id=1, source_target_pairs={{0,8},{4,12},{8,0},{12,4},{16,24},{20,28},{24,16},{28,20},{1,9},{5... | collective-permute-start | bytes 1572872 | tf_op jit(solution)/shard_map/ppermute | solution.py:29
  68.5 19.9 %collective-permute-start.25 = (bf16[512,512]{1,0:T(8,128)(2,1)S(1)}, bf16[512,512]{1,0:T(8,128)(2,1)S(1)}, u32[]{:S(2)}, u32[]{:S(2)}) collective-permute-start(bf16[512,512]{1,0:T(8,128)(2,1)S(1)} %merge_z.1.refs_0_), channel_id=1, source_target_pairs={{0,16},{4,20},{8,24},{12,28},{16,0},{20,4},{24,8},{28,12},{1,17},{... | collective-permute-start | bytes 1572872 | tf_op jit(solution)/shard_map/ppermute | solution.py:29
  75.1 11.8 %collective-permute-start.22 = (bf16[2,544,128]{2,1,0:T(8,128)(2,1)S(1)}, bf16[2,544,128]{2,1,0:T(8,128)(2,1)S(1)}, u32[]{:S(2)}, u32[]{:S(2)}) collective-permute-start(bf16[2,544,128]{2,1,0:T(8,128)(2,1)S(1)} %get-tuple-element.195.refs_0_), channel_id=1, source_target_pairs={{0,8},{4,12},{8,0},{12,4},{16,24},{20,28},{24,16},{28,20},{1,9},{5... | collective-permute-start | bytes 835592 | tf_op jit(solution)/shard_map/ppermute | solution.py:29
  75.5 12.9 %collective-permute-start.23 = (bf16[2,544,128]{2,1,0:T(8,128)(2,1)S(1)}, bf16[2,544,128]{2,1,0:T(8,128)(2,1)S(1)}, u32[]{:S(2)}, u32[]{:S(2)}) collective-permute-start(bf16[2,544,128]{2,1,0:T(8,128)(2,1)S(1)} %get-tuple-element.195.refs_0_), channel_id=1, source_target_pairs={{0,16},{4,20},{8,24},{12,28},{16,0},{20,4},{24,8},{28,12},{1,17},{... | collective-permute-start | bytes 835592 | tf_op jit(solution)/shard_map/ppermute | solution.py:29
  88.4 9.6 %collective-permute-start.31 = (bf16[2,544,128]{2,1,0:T(8,128)(2,1)S(1)}, bf16[2,544,128]{2,1,0:T(8,128)(2,1)S(1)}, u32[]{:S(2)}, u32[]{:S(2)}) collective-permute-start(bf16[2,544,128]{2,1,0:T(8,128)(2,1)S(1)} %get-tuple-element.196.refs_1_), channel_id=1, source_target_pairs={{0,8},{4,12},{8,0},{12,4},{16,24},{20,28},{24,16},{28,20},{1,9},{5... | collective-permute-start | bytes 835592 | tf_op jit(solution)/shard_map/ppermute | solution.py:29
  89.0 9.6 %collective-permute-start.32 = (bf16[2,544,128]{2,1,0:T(8,128)(2,1)S(1)}, bf16[2,544,128]{2,1,0:T(8,128)(2,1)S(1)}, u32[]{:S(2)}, u32[]{:S(2)}) collective-permute-start(bf16[2,544,128]{2,1,0:T(8,128)(2,1)S(1)} %get-tuple-element.196.refs_1_), channel_id=1, source_target_pairs={{0,16},{4,20},{8,24},{12,28},{16,0},{20,4},{24,8},{28,12},{1,17},{... | collective-permute-start | bytes 835592 | tf_op jit(solution)/shard_map/ppermute | solution.py:29
  89.3 14.3 %collective-permute-start.35 = (bf16[256,512]{1,0:T(8,128)(2,1)S(1)}, bf16[256,512]{1,0:T(8,128)(2,1)S(1)}, u32[]{:S(2)}, u32[]{:S(2)}) collective-permute-start(bf16[256,512]{1,0:T(8,128)(2,1)S(1)} %slice.26), channel_id=1, source_target_pairs={{0,8},{4,12},{8,0},{12,4},{16,24},{20,28},{24,16},{28,20},{1,9},{5... | collective-permute-start | bytes 786440 | tf_op jit(solution)/shard_map/ppermute | solution.py:29
  90.8 13.4 %collective-permute-start.36 = (bf16[256,512]{1,0:T(8,128)(2,1)S(1)}, bf16[256,512]{1,0:T(8,128)(2,1)S(1)}, u32[]{:S(2)}, u32[]{:S(2)}) collective-permute-start(bf16[256,512]{1,0:T(8,128)(2,1)S(1)} %slice.27), channel_id=1, source_target_pairs={{0,16},{4,20},{8,24},{12,28},{16,0},{20,4},{24,8},{28,12},{1,17},{... | collective-permute-start | bytes 786440 | tf_op jit(solution)/shard_map/ppermute | solution.py:29
  95.0 13.1 %collective-permute-start.33 = (bf16[2,544,128]{2,1,0:T(8,128)(2,1)S(1)}, bf16[2,544,128]{2,1,0:T(8,128)(2,1)S(1)}, u32[]{:S(2)}, u32[]{:S(2)}) collective-permute-start(bf16[2,544,128]{2,1,0:T(8,128)(2,1)S(1)} %collective-permute-done.23.refs_4_), channel_id=1, source_target_pairs={{0,8},{4,12},{8,0},{12,4},{16,24},{20,28},{24,16},{28,20},{1,9},{5... | collective-permute-start | bytes 835592 | tf_op jit(solution)/shard_map/ppermute | solution.py:29
  98.6 9.8 %collective-permute-start.34 = (bf16[2,544,128]{2,1,0:T(8,128)(2,1)S(1)}, bf16[2,544,128]{2,1,0:T(8,128)(2,1)S(1)}, u32[]{:S(2)}, u32[]{:S(2)}) collective-permute-start(bf16[2,544,128]{2,1,0:T(8,128)(2,1)S(1)} %collective-permute-done.31.refs_3_), channel_id=1, source_target_pairs={{0,16},{4,20},{8,24},{12,28},{16,0},{20,4},{24,8},{28,12},{1,17},{... | collective-permute-start | bytes 835592 | tf_op jit(solution)/shard_map/ppermute | solution.py:29
  110.6 2.2 %collective-permute-start.37 = (bf16[512,640]{1,0:T(8,128)(2,1)S(1)}, bf16[512,640]{1,0:T(8,128)(2,1)S(1)}, u32[]{:S(2)}, u32[]{:S(2)}) collective-permute-start(bf16[512,640]{1,0:T(8,128)(2,1)S(1)} %get-tuple-element.212), channel_id=1, source_target_pairs={{0,4},{4,0},{8,12},{12,8},{16,20},{20,16},{24,28},{28,24},{1,5},{5... | collective-permute-start | bytes 1966088 | tf_op jit(solution)/shard_map/ppermute | solution.py:29
  115.3 14.7 %collective-permute-start.38 = (bf16[128,2176]{1,0:T(8,128)(2,1)S(1)}, bf16[128,2176]{1,0:T(8,128)(2,1)S(1)}, u32[]{:S(2)}, u32[]{:S(2)}) collective-permute-start(bf16[128,2176]{1,0:T(8,128)(2,1)S(1)} %get-tuple-element.218), channel_id=1, source_target_pairs={{0,1},{1,0},{2,3},{3,2},{4,5},{5,4},{6,7},{7,6},{8,9},{9,8},{10,11... | collective-permute-start | bytes 1671176 | tf_op jit(solution)/shard_map/ppermute | solution.py:537
  130.9 15.6 %collective-permute-start.39 = (bf16[128,2176]{1,0:T(8,128)(2,1)S(1)}, bf16[128,2176]{1,0:T(8,128)(2,1)S(1)}, u32[]{:S(2)}, u32[]{:S(2)}) collective-permute-start(bf16[128,2176]{1,0:T(8,128)(2,1)S(1)} %add_far.1), channel_id=1, source_target_pairs={{0,1},{3,2},{1,3},{2,0},{4,5},{7,6},{5,7},{6,4},{8,9},{11,10},{9,1... | collective-permute-start | bytes 1671176 | tf_op jit(solution)/shard_map/ppermute | solution.py:537
  131.0 25.7 %collective-permute-start.40 = (bf16[128,2176]{1,0:T(8,128)(2,1)S(1)}, bf16[128,2176]{1,0:T(8,128)(2,1)S(1)}, u32[]{:S(2)}, u32[]{:S(2)}) collective-permute-start(bf16[128,2176]{1,0:T(8,128)(2,1)S(1)} %get-tuple-element.227.own), channel_id=1, source_target_pairs={{0,1},{3,2},{4,5},{7,6},{8,9},{11,10},{12,13},{15,14},{16,17},{19,... | collective-permute-start | bytes 1671176 | tf_op jit(solution)/shard_map/ppermute | solution.py:537
  147.3 13.1 %collective-permute-start.41 = (bf16[128,2176]{1,0:T(8,128)(2,1)S(1)}, bf16[128,2176]{1,0:T(8,128)(2,1)S(1)}, u32[]{:S(2)}, u32[]{:S(2)}) collective-permute-start(bf16[128,2176]{1,0:T(8,128)(2,1)S(1)} %add_mid.1), channel_id=1, source_target_pairs={{1,2},{2,1},{0,0},{3,3},{5,6},{6,5},{4,4},{7,7},{9,10},{10,9},{8,8... | collective-permute-start | bytes 1671176 | tf_op jit(solution)/shard_map/ppermute | solution.py:537
  149.2 1.6 collective-permute-start.42
